TPU v7x, 128 devices: a whole 4x4x4 slice. The times are simulated.
128 devices in a mesh: shard: 32 (over y, z, core), grp: 4 (over x).
Axes of the slice: x: 4, y: 4, z: 4, core: 2. Of those that a mesh axis runs over, the one named last changes fastest.
Arguments:
- corpus: float32 [8192, 8, 768], P(('shard', 'grp')), may hold values from -6 to 6
- block_rows: int32 [8192], P(('shard', 'grp')), may hold values from 1 to 8
- targets: int32 [8192, 1], P(('shard', 'grp')), may hold values from 0 to 31; in each aligned block of 64 rows (0 to 63, 64 to 127, ...) at most 4 rows name the same one
- assign: int32 [8192, 8], P(('shard', 'grp')), may hold values from 0 to 4095
- codes: int32 [8192, 8, 96], P(('shard', 'grp')), may hold values from 0 to 255
- centroids: float32 [4096, 768], P('shard'), may hold values from -4 to 4
- codebook: float32 [256, 768], replicated, may hold values from -4 to 4
Outputs:
- new_centroids: float32 [4096, 768], P('shard')
- moved_error: bfloat16 [16384, 8, 768], P(('shard', 'grp'))
- new_codebook: float32 [256, 768], replicated
Inputs may be any that keep to these rules, and one draw needn't show every extreme that they name: `targets`: among the 64 blocks of one device no shard is named more than 4 times, and some device names one shard exactly 4 times.
All inputs are finite; a program needn't handle non-finite values.
Results may differ from a plain program's by a relative error of at most 0.001.
Values sent between devices are 32-bit elements; how exact they have to be, the bound alone decides.
No kernel may reach another device: no remote copies, remote signals or barrier semaphores. Data moves between devices by JAX's collectives and lax.ppermute only.
A program may use at most 192 MiB of HBM per device.

v0:
```python
import jax
import jax.numpy as jnp
from jax import lax
from jax.sharding import PartitionSpec as P

prior_weight = 8.0


def slot_ranks(dest):
    count = dest.shape[0]
    order = jnp.arange(count, dtype=jnp.int32)
    same = (dest[:, None] == dest[None, :]) & (order[None, :] < order[:, None])
    return jnp.sum(same.astype(jnp.int32), axis=1)


def row_weights(counts, width):
    return (jnp.arange(width, dtype=jnp.int32)[None, :] < counts[:, None]).astype(jnp.float32)


def centroid_terms(rows, labels, weight, clusters):
    flat_weight = weight.reshape(-1)
    ids = labels.reshape(-1)
    sums = jax.ops.segment_sum(
        rows.reshape(-1, rows.shape[-1]) * flat_weight[:, None], ids, num_segments=clusters
    )
    counts = jax.ops.segment_sum(flat_weight, ids, num_segments=clusters)
    return (sums, counts)


def group_blocks(blocks, width):
    limit = max(1, 256 // width)
    step = 1
    for trial in range(1, blocks + 1):
        if blocks % trial == 0 and trial <= limit:
            step = trial
    return step


def one_hot_codes(labels, books):
    return (labels[:, :, None] == jnp.arange(books, dtype=jnp.int32)[None, None, :]).astype(
        jnp.float32
    )


def code_terms(resid, words, weight, books):
    blocks, width, feat = resid.shape
    subs = words.shape[-1]
    sub_width = feat // subs
    step = group_blocks(blocks, width)
    groups = blocks // step
    rows = step * width
    resid_groups = resid.reshape(groups, rows, subs, sub_width)
    word_groups = words.reshape(groups, rows, subs)
    weight_groups = weight.reshape(groups, rows)

    def add_group(carry, parts):
        piece, labels, row_weight = parts
        table = one_hot_codes(labels, books) * row_weight[:, None, None]
        part_sum = jnp.einsum("rmc,rms->mcs", table, piece, precision=lax.Precision.HIGHEST)
        return ((carry[0] + part_sum, carry[1] + jnp.sum(table, axis=0)), None)

    start = (
        jnp.zeros((subs, books, sub_width), jnp.float32),
        jnp.zeros((subs, books), jnp.float32),
    )
    totals, unused = lax.scan(add_group, start, (resid_groups, word_groups, weight_groups))
    return totals


def look_up_words(words, fresh_book, width):
    blocks = words.shape[0]
    subs, books, sub_width = fresh_book.shape
    step = group_blocks(blocks, width)
    groups = blocks // step
    word_groups = words.reshape(groups, step * width, subs)

    def pick(labels):
        table = one_hot_codes(labels, books)
        return jnp.einsum("rmc,mcs->rms", table, fresh_book, precision=lax.Precision.HIGHEST)

    picked = lax.map(pick, word_groups)
    return picked.reshape(blocks, width, subs * sub_width)


def local(corpus, block_rows, targets, assign, codes, centroids, codebook):
    shards = lax.axis_size("shard")
    blocks, width, feat = corpus.shape
    owned = centroids.shape[0]
    clusters = owned * shards
    books = codebook.shape[0]
    subs = codes.shape[-1]
    sub_width = feat // subs
    cap = max(2, (2 * blocks + shards - 1) // shards)
    total = shards * cap
    dest = targets[:, 0]
    slot = dest * cap + slot_ranks(dest)
    send_rows = jnp.zeros((total, width, feat), jnp.float32).at[slot].set(corpus)
    send_count = jnp.zeros((total,), jnp.int32).at[slot].set(block_rows)
    send_assign = jnp.zeros((total, width), jnp.int32).at[slot].set(assign)
    send_codes = jnp.zeros((total, width, subs), jnp.int32).at[slot].set(codes)
    moved, moved_count, moved_assign, moved_codes = (
        lax.all_to_all(send_rows, "shard", split_axis=0, concat_axis=0, tiled=True),
        lax.all_to_all(send_count, "shard", split_axis=0, concat_axis=0, tiled=True),
        lax.all_to_all(send_assign, "shard", split_axis=0, concat_axis=0, tiled=True),
        lax.all_to_all(send_codes, "shard", split_axis=0, concat_axis=0, tiled=True),
    )
    moved_weight = row_weights(moved_count, width)
    sums, counts = centroid_terms(moved, moved_assign, moved_weight, clusters)
    part_sums, part_counts = (
        lax.psum_scatter(sums, "shard", scatter_dimension=0, tiled=True),
        lax.psum_scatter(counts, "shard", scatter_dimension=0, tiled=True),
    )
    part_sums, part_counts = lax.psum((part_sums, part_counts), "grp")
    new_centroids = (part_sums + prior_weight * centroids) / (part_counts[:, None] + prior_weight)
    table = lax.all_gather(new_centroids, "shard", axis=0, tiled=True)
    moved_resid = moved - jnp.take(table, moved_assign, axis=0)
    csum, ccount = code_terms(moved_resid, moved_codes, moved_weight, books)
    csum, ccount = lax.psum((csum.reshape(subs, books * sub_width), ccount), ("shard", "grp"))
    old_book = codebook.reshape(books, subs, sub_width).transpose(1, 0, 2)
    fresh_book = (csum.reshape(subs, books, sub_width) + prior_weight * old_book) / (
        ccount.reshape(subs, books, 1) + prior_weight
    )
    words = look_up_words(moved_codes, fresh_book, width)
    moved_error = ((moved_resid - words) * moved_weight[:, :, None]).astype(jnp.bfloat16)
    new_codebook = fresh_book.transpose(1, 0, 2).reshape(books, feat)
    return (new_centroids, moved_error, new_codebook)


def solution(mesh):
    in_specs = (
        P(("shard", "grp"), None, None),
        P(("shard", "grp")),
        P(("shard", "grp"), None),
        P(("shard", "grp"), None),
        P(("shard", "grp"), None, None),
        P("shard", None),
        P(),
    )
    out_specs = (P("shard", None), P(("shard", "grp"), None, None), P())
    return jax.shard_map(local, mesh=mesh, in_specs=in_specs, out_specs=out_specs, check_vma=False)
```

profile of v0, /device:TPU:1, one launch (start us, length us, event | category | flops | bytes accessed | tf_op | source)
XLA Modules:
  0.0 877.9 jit_solution(4563956084289222034)
XLA Ops:
  10.4 9.6 %all-to-all-start.2 = ((s32[32,4,1]{1,2,0:T(1,128)}), s32[32,4,1]{1,2,0:T(1,128)S(1)}, u32[]{:S(2)}, u32[]{:S(2)}) async-start(s32[32,4,1]{1,2,0:T(1,128)} %bitcast.8), calls=%async_computation.2 | async-start | bytes 32768 | tf_op jit(solution)/shard_map/all_to_all | solution.py:103
  31.2 6.4 scatter_fusion
  39.3 7.5 all-to-all-start.1
  48.5 38.1 %all-to-all-done.1 = f32[128,8,768]{2,1,0:T(8,128)S(1)} async-done(((f32[128,8,768]{2,1,0:T(8,128)}), f32[128,8,768]{2,1,0:T(8,128)S(1)}, u32[]{:S(2)}, u32[]{:S(2)}) %all-to-all-start.1) | async-done | bytes 3145760 | tf_op jit(solution)/shard_map/all_to_all | solution.py:102
  86.6 13.1 %scatter_custom_fusion.3 = f32[4096,768]{1,0:T(8,128)} fusion(s32[1024]{0:T(1024)S(1)} %reshape.177, f32[]{:T(128)} %constant.22.clone.1, f32[128,8,768]{2,1,0:T(8,128)S(1)} %all-to-all-done.1, f32[1024]{0:T(1024)S(1)} %reshape.187), kind=kCustom, calls=%fused_computation.28 | custom fusion | flops 1572864 | bytes 15732740 | tf_op jit(solution)/shard_map/scatter-add | solution.py:23
  99.7 102.1 %reduce-scatter.2.cloned.1.call-done = f32[128,768]{1,0:T(8,128)} async-done(((f32[4096,768]{1,0:T(8,128)}), f32[128,768]{1,0:T(8,128)}) %reduce-scatter.2.cloned.1.call-update) | async-done | bytes 393232 | tf_op jit(solution)/shard_map/reduce_scatter | solution.py:110
  209.5 120.9 %all-reduce = f32[4096]{0:T(1024)S(1)} all-reduce(f32[4096]{0:T(1024)S(1)} %scatter_custom_fusion.4), channel_id=3, replica_groups=mesh['shard'=32,'grp'=4] {'shard'}, use_global_device_ids=true, to_apply=%region_8.0.clone | all-reduce | flops 4096 | bytes 32768
  330.5 8.6 psum.29
  341.9 6.9 scatter_fusion.1
  348.8 11.7 %all-to-all-start.3 = ((s32[128,8,96]{2,1,0:T(8,128)}), s32[128,8,96]{2,1,0:T(8,128)}, u32[]{:S(2)}, u32[]{:S(2)}) async-start(s32[128,8,96]{2,1,0:T(8,128)} %scatter_fusion.1), calls=%async_computation.4 | async-start | bytes 1048576 | tf_op jit(solution)/shard_map/all_to_all | solution.py:105
  361.8 11.2 %all-to-all-done.3 = s32[128,8,96]{2,1,0:T(8,128)} async-done(((s32[128,8,96]{2,1,0:T(8,128)}), s32[128,8,96]{2,1,0:T(8,128)}, u32[]{:S(2)}, u32[]{:S(2)}) %all-to-all-start.3) | async-done | bytes 393248 | tf_op jit(solution)/shard_map/all_to_all | solution.py:105
  374.3 36.1 %all-gather.2.cloned.1.call-done = f32[4096,768]{1,0:T(8,128)} async-done(((f32[128,768]{1,0:T(8,128)}), f32[4096,768]{1,0:T(8,128)}) %all-gather.2.cloned.1.call-update) | async-done | bytes 12582928 | tf_op jit(solution)/shard_map/all_gather | solution.py:115
  410.4 10.4 %gather_fusion = f32[1024,768]{1,0:T(8,128)} fusion(f32[4096,768]{1,0:T(8,128)} %all-gather.2.cloned.1.call-done, s32[1024]{0:T(1024)S(1)} %broadcast_clamp_fusion), kind=kCustom, calls=%fused_computation | custom fusion | bytes 6295552 | tf_op jit(solution)/shard_map/jit(_take)/gather | solution.py:116
  424.8 31.0 %reshape.136 = f32[4,256,96,8]{3,2,1,0:T(8,128)} reshape(f32[128,8,768]{2,1,0:T(8,128)} %fusion.18) | data formatting | bytes 6291456 | tf_op jit(solution)/shard_map/reshape | solution.py:52
  455.8 34.8 %copy.32 = f32[4,256,96,8]{1,3,2,0:T(8,128)} copy(f32[4,256,96,8]{3,2,1,0:T(8,128)} %reshape.136) | data formatting | bytes 6291456
  490.6 97.4 %while.24 = (s32[]{:T(128)}, f32[96,256,8]{1,2,0:T(8,128)S(1)}, f32[96,256]{1,0:T(8,128)S(1)}, s32[4,256,96]{1,2,0:T(8,128)S(1)}, f32[4,256]{1,0:T(4,128)S(1)}, ...) while((s32[]{:T(128)}, f32[96,256,8]{1,2,0:T(8,128)S(1)}, f32[96,256]{1,0:T(8,128)S(1)}, ...), condition=%wide.region_13.14_spmd.clone, body=%wide.region_11.0_spmd.clone.sunk | while | flops 635854848 | bytes 3150440 | solution.py:66
  490.6 16.2 %fusion.41 = f32[96,256,8]{1,2,0:T(8,128)S(1)} fusion(f32[256]{0:T(256)S(1)} %bitcast.70, s32[256,96]{0,1:T(8,128)S(1)} %dynamic-slice_bitcast_fusion.5, f32[96,256,8]{1,2,0:T(8,128)S(1)} %get-tuple-element.220, f32[4,256,96,8]{1,3,2,0:T(8,128)} %get-tuple-element.232, s32[]{:T(128)} %get-tuple-element.219, pred[]{:T(512)S(6)} %compare.3), kind=kOutput, calls=%fused_computation.20.clone.1 | convolution fusion | flops 616955904 | bytes 2459137 | tf_op jit(solution)/shard_map/while/body/eval_jaxpr/rmc,rms->mcs/dot_general | solution.py:59
  506.8 8.1 select_reduce_fusion.2
  515.0 16.1 %fusion.41 = f32[96,256,8]{1,2,0:T(8,128)S(1)} fusion(f32[256]{0:T(256)S(1)} %bitcast.70, s32[256,96]{0,1:T(8,128)S(1)} %dynamic-slice_bitcast_fusion.5, f32[96,256,8]{1,2,0:T(8,128)S(1)} %get-tuple-element.220, f32[4,256,96,8]{1,3,2,0:T(8,128)} %get-tuple-element.232, s32[]{:T(128)} %get-tuple-element.219, pred[]{:T(512)S(6)} %compare.3), kind=kOutput, calls=%fused_computation.20.clone.1 | convolution fusion | flops 616955904 | bytes 2459137 | tf_op jit(solution)/shard_map/while/body/eval_jaxpr/rmc,rms->mcs/dot_general | solution.py:59
  531.1 8.1 select_reduce_fusion.2
  539.2 16.1 %fusion.41 = f32[96,256,8]{1,2,0:T(8,128)S(1)} fusion(f32[256]{0:T(256)S(1)} %bitcast.70, s32[256,96]{0,1:T(8,128)S(1)} %dynamic-slice_bitcast_fusion.5, f32[96,256,8]{1,2,0:T(8,128)S(1)} %get-tuple-element.220, f32[4,256,96,8]{1,3,2,0:T(8,128)} %get-tuple-element.232, s32[]{:T(128)} %get-tuple-element.219, pred[]{:T(512)S(6)} %compare.3), kind=kOutput, calls=%fused_computation.20.clone.1 | convolution fusion | flops 616955904 | bytes 2459137 | tf_op jit(solution)/shard_map/while/body/eval_jaxpr/rmc,rms->mcs/dot_general | solution.py:59
  555.4 8.1 select_reduce_fusion.2
  563.5 16.1 %fusion.41 = f32[96,256,8]{1,2,0:T(8,128)S(1)} fusion(f32[256]{0:T(256)S(1)} %bitcast.70, s32[256,96]{0,1:T(8,128)S(1)} %dynamic-slice_bitcast_fusion.5, f32[96,256,8]{1,2,0:T(8,128)S(1)} %get-tuple-element.220, f32[4,256,96,8]{1,3,2,0:T(8,128)} %get-tuple-element.232, s32[]{:T(128)} %get-tuple-element.219, pred[]{:T(512)S(6)} %compare.3), kind=kOutput, calls=%fused_computation.20.clone.1 | convolution fusion | flops 616955904 | bytes 2459137 | tf_op jit(solution)/shard_map/while/body/eval_jaxpr/rmc,rms->mcs/dot_general | solution.py:59
  579.6 8.1 select_reduce_fusion.2
  589.3 145.5 %all-reduce.7.cloned.1.call-done = (f32[96,256,8]{1,2,0:T(8,128)}, f32[96,256]{1,0:T(8,128)}) async-done(((f32[96,256,8]{1,2,0:T(8,128)}, f32[96,256]{1,0:T(8,128)}), (f32[96,256,8]{1,2,0:T(8,128)}, f32[96,256]{1,0:T(8,128)})) %all-reduce.7.cloned.1.call-update) | async-done | bytes 884752 | tf_op jit(solution)/shard_map/psum | solution.py:118
  739.2 54.8 %while.23 = (s32[]{:T(128)}, f32[4,256,96,8]{1,3,2,0:T(8,128)}, s32[4,256,96]{1,2,0:T(8,128)S(1)}, f32[96,256,8]{1,2,0:T(8,128)}, s32[]{:T(128)}) while((s32[]{:T(128)}, f32[4,256,96,8]{1,3,2,0:T(8,128)}, s32[4,256,96]{1,2,0:T(8,128)S(1)}, f32[96,256,8]{1,2,0:T(8,128)}, s32[]{:T(128)}) %tuple.64), condition=%wide.region_17.18_spmd, body=%wide.region_16.17_spmd.sunk | while | flops 610271232 | bytes 1868353 | solution.py:81
  739.2 13.7 %fusion.38 = f32[4,256,96,8]{1,3,2,0:T(8,128)} fusion(f32[4,256,96,8]{1,3,2,0:T(8,128)} %get-tuple-element.241, s32[]{:T(128)} %get-tuple-element.240, f32[96,256,8]{1,2,0:T(8,128)} %get-tuple-element.248, s32[256,96]{0,1:T(8,128)S(1)} %dynamic-slice_bitcast_fusion.4), kind=kOutput, calls=%fused_computation.11.clone.1 | convolution fusion | flops 610271232 | bytes 1671680 | tf_op jit(solution)/shard_map/while/body/eval_jaxpr/rmc,mcs->rms/dot_general | solution.py:79
  752.9 13.7 %fusion.38 = f32[4,256,96,8]{1,3,2,0:T(8,128)} fusion(f32[4,256,96,8]{1,3,2,0:T(8,128)} %get-tuple-element.241, s32[]{:T(128)} %get-tuple-element.240, f32[96,256,8]{1,2,0:T(8,128)} %get-tuple-element.248, s32[256,96]{0,1:T(8,128)S(1)} %dynamic-slice_bitcast_fusion.4), kind=kOutput, calls=%fused_computation.11.clone.1 | convolution fusion | flops 610271232 | bytes 1671680 | tf_op jit(solution)/shard_map/while/body/eval_jaxpr/rmc,mcs->rms/dot_general | solution.py:79
  766.6 13.7 %fusion.38 = f32[4,256,96,8]{1,3,2,0:T(8,128)} fusion(f32[4,256,96,8]{1,3,2,0:T(8,128)} %get-tuple-element.241, s32[]{:T(128)} %get-tuple-element.240, f32[96,256,8]{1,2,0:T(8,128)} %get-tuple-element.248, s32[256,96]{0,1:T(8,128)S(1)} %dynamic-slice_bitcast_fusion.4), kind=kOutput, calls=%fused_computation.11.clone.1 | convolution fusion | flops 610271232 | bytes 1671680 | tf_op jit(solution)/shard_map/while/body/eval_jaxpr/rmc,mcs->rms/dot_general | solution.py:79
  780.2 13.7 %fusion.38 = f32[4,256,96,8]{1,3,2,0:T(8,128)} fusion(f32[4,256,96,8]{1,3,2,0:T(8,128)} %get-tuple-element.241, s32[]{:T(128)} %get-tuple-element.240, f32[96,256,8]{1,2,0:T(8,128)} %get-tuple-element.248, s32[256,96]{0,1:T(8,128)S(1)} %dynamic-slice_bitcast_fusion.4), kind=kOutput, calls=%fused_computation.11.clone.1 | convolution fusion | flops 610271232 | bytes 1671680 | tf_op jit(solution)/shard_map/while/body/eval_jaxpr/rmc,mcs->rms/dot_general | solution.py:79
  793.9 38.2 %copy.35 = f32[4,256,96,8]{3,2,1,0:T(8,128)} copy(f32[4,256,96,8]{1,3,2,0:T(8,128)} %get-tuple-element.60) | data formatting | bytes 6291456 | tf_op jit(solution)/shard_map/while | solution.py:81
  832.2 35.2 %reshape.139 = f32[128,8,768]{2,1,0:T(8,128)} reshape(f32[4,256,96,8]{3,2,1,0:T(8,128)} %copy.35) | data formatting | bytes 6291456 | tf_op jit(solution)/shard_map/reshape | solution.py:82
  (97 shorter events, 44.0 us)
Async XLA Ops:
  10.4 16.5 %all-to-all-start.2 = ((s32[32,4,1]{1,2,0:T(1,128)}), s32[32,4,1]{1,2,0:T(1,128)S(1)}, u32[]{:S(2)}, u32[]{:S(2)}) async-start(s32[32,4,1]{1,2,0:T(1,128)} %bitcast.8), calls=%async_computation.2 | async-start | bytes 32768 | tf_op jit(solution)/shard_map/all_to_all | solution.py:103
  26.8 12.5 %all-to-all-start = ((s32[32,4,8]{2,1,0:T(4,128)}), s32[32,4,8]{2,1,0:T(4,128)S(1)}, u32[]{:S(2)}, u32[]{:S(2)}) async-start(s32[32,4,8]{2,1,0:T(4,128)} %bitcast.6), calls=%async_computation | async-start | bytes 131072 | tf_op jit(solution)/shard_map/all_to_all | solution.py:104
  37.7 1.7 copy-start.2
  39.3 47.3 %all-to-all-start.1 = ((f32[128,8,768]{2,1,0:T(8,128)}), f32[128,8,768]{2,1,0:T(8,128)S(1)}, u32[]{:S(2)}, u32[]{:S(2)}) async-start(f32[128,8,768]{2,1,0:T(8,128)} %copy-done.2), calls=%async_computation.1 | async-start | bytes 6291456 | tf_op jit(solution)/shard_map/all_to_all | solution.py:102
  46.8 155.0 %reduce-scatter.2.cloned.1.call-start = ((), (), s32[]{:S(2)}) async-start(), calls=%async_computation.5 | async-start | bytes 12976128 | tf_op jit(solution)/shard_map/reduce_scatter | solution.py:110
  48.3 51.4 %copy-start.9 = (f32[128,8]{1,0:T(8,128)}, f32[128,8]{1,0:T(8,128)S(1)}, u32[]{:S(2)}) copy-start(f32[128,8]{1,0:T(8,128)S(1)} %fusion.21) | copy-start | bytes 12292
  86.6 334.2 %copy-start = (f32[128,8,768]{2,1,0:T(8,128)}, f32[128,8,768]{2,1,0:T(8,128)S(1)}, u32[]{:S(2)}) copy-start(f32[128,8,768]{2,1,0:T(8,128)S(1)} %all-to-all-done.1) | copy-start | bytes 9437188
  99.7 102.3 %copy-start.13 = (u32[128]{0:T(128)S(1)}, u32[128]{0:T(128)}, u32[]{:S(2)}) copy-start(u32[128]{0:T(128)} %constant.66) | copy-start | bytes 1540
  99.7 242.2 %copy-start.11 = (s32[64,8,96]{2,1,0:T(8,128)S(1)}, s32[64,8,96]{2,1,0:T(8,128)}, u32[]{:S(2)}) copy-start(s32[64,8,96]{2,1,0:T(8,128)} %param.15) | copy-start | bytes 589828
  99.7 239.4 %all-reduce.5.cloned.1.call-start = ((), (), s32[]{:S(2)}) async-start(), calls=%async_computation.6 | async-start | bytes 786432 | tf_op jit(solution)/shard_map/psum | solution.py:113
  201.9 208.5 %all-gather.2.cloned.1.call-start = ((), (), s32[]{:S(2)}) async-start(), calls=%async_computation.7 | async-start | bytes 12976128 | tf_op jit(solution)/shard_map/all_gather | solution.py:115
  348.8 24.3 %all-to-all-start.3 = ((s32[128,8,96]{2,1,0:T(8,128)}), s32[128,8,96]{2,1,0:T(8,128)}, u32[]{:S(2)}, u32[]{:S(2)}) async-start(s32[128,8,96]{2,1,0:T(8,128)} %scatter_fusion.1), calls=%async_computation.4 | async-start | bytes 1048576 | tf_op jit(solution)/shard_map/all_to_all | solution.py:105
  360.4 374.3 %all-reduce.7.cloned.1.call-start = ((), (), s32[]{:S(2)}) async-start(), calls=%async_computation.8 | async-start | bytes 1769472 | tf_op jit(solution)/shard_map/psum | solution.py:118
  455.8 34.8 %copy-start.3 = (f32[96,256]{1,0:T(8,128)S(1)}, f32[96,256]{1,0:T(8,128)}, u32[]{:S(2)}) copy-start(f32[96,256]{1,0:T(8,128)} %custom-call.1) | copy-start | bytes 294916
  455.8 34.8 %copy-start.7 = (f32[96,256,8]{1,2,0:T(8,128)S(1)}, f32[96,256,8]{1,2,0:T(8,128)}, u32[]{:S(2)}) copy-start(f32[96,256,8]{1,2,0:T(8,128)} %custom-call) | copy-start | bytes 2359300
  490.6 98.4 %copy-start.6 = (f32[256,768]{1,0:T(8,128)S(1)}, f32[256,768]{1,0:T(8,128)}, u32[]{:S(2)}) copy-start(f32[256,768]{1,0:T(8,128)} %param.17) | copy-start | bytes 2359300
  588.0 0.6 copy-start.4
  588.0 0.9 copy-start.8
  734.8 2.2 copy-start.5
  832.2 35.2 %copy-start.1 = (f32[128,8,768]{2,1,0:T(8,128)S(1)}, f32[128,8,768]{2,1,0:T(8,128)}, u32[]{:S(2)}) copy-start(f32[128,8,768]{2,1,0:T(8,128)} %copy-done) | copy-start | bytes 9437188
  832.2 35.2 %copy-start.10 = (f32[128,8]{1,0:T(8,128)S(1)}, f32[128,8]{1,0:T(8,128)}, u32[]{:S(2)}) copy-start(f32[128,8]{1,0:T(8,128)} %copy-done.9) | copy-start | bytes 12292
  832.2 35.2 %copy-start.12 = (pred[128,8]{1,0:T(8,128)(4,1)S(1)}, pred[128,8]{1,0:T(8,128)(4,1)}, u32[]{:S(2)}) copy-start(pred[128,8]{1,0:T(8,128)(4,1)} %compare_and_fusion) | copy-start | bytes 3076
Sparse Core Ops, SparseCore 0:
  99.8 101.9 reduce-scatter.1
  204.3 40.4 all-reduce.4
  341.2 69.1 all-gather.1
  589.0 145.6 all-reduce.6
where the time goes:
time: 880 us; the launch traced here: 878 us
  waiting for transfers between devices  338 us (38%)
  local copies, waits for them, and re-layouts  175 us (20%)
  blocking collectives  130 us (15%)
  matrix products  119 us (14%)
  other arithmetic  68 us (8%)
  starting transfers between devices  33.3 us (4%)
  between operations  14.7 us (2%)
    psum x1, waiting for transfers between devices, local(): lax.psum((csum.reshape(subs, books * sub_width), ccount), ('shard', 'grp'))  145 us
    unnamed x1, blocking collectives  121 us
    reduce_scatter x1, waiting for transfers between devices, local(): lax.psum_scatter(sums, 'shard', scatter_dimension=0, tiled=True)  102 us
    dot_general x4, matrix products, add_group(): jnp.einsum('rmc,rms->mcs', table, piece, precision=lax.Precision.HIGHEST)  64.5 us
    dot_general x4, matrix products, pick(): jnp.einsum('rmc,mcs->rms', table, fresh_book, precision=lax.Precision.HIG...  54.7 us
    unnamed x33, local copies, waits for them, and re-layouts  39.9 us
    while x2, local copies, waits for them, and re-layouts, look_up_words(): picked = lax.map(pick, word_groups)  39.5 us
    all_to_all x1, waiting for transfers between devices, local(): lax.all_to_all(send_rows, 'shard', split_axis=0, concat_axis=0, tiled=True)  38.1 us
  transfers between devices with their start and end apart: 8, of which 6 were waited for; matrix products, arithmetic and copies ran while one was open for 3% of the time, Pallas kernels for 0%

commit v1 on v0

v1 whole, which is shorter than its diff:
```python
import jax
import jax.numpy as jnp
from jax import lax
from jax.experimental import pallas as pl
from jax.experimental.pallas import tpu as pltpu
from jax.sharding import PartitionSpec as P

PRIOR = 8.0
BOTH = ("shard", "grp")
F32 = jnp.float32
BF16 = jnp.bfloat16
VMEM_LIMIT = 56 * 1024 * 1024

CH = 40
FIRST = (0, 0, 1, 2)
SECOND = (0, 1, 2, 2)


def call(body, out, scratch=(), flops=0, moved=0):
    return pl.pallas_call(
        body,
        out_shape=out,
        scratch_shapes=list(scratch),
        compiler_params=pltpu.CompilerParams(vmem_limit_bytes=VMEM_LIMIT),
        cost_estimate=pl.CostEstimate(flops=flops, bytes_accessed=moved, transcendentals=0),
    )


def nt(a, b):
    return lax.dot_general(a, b, (((1,), (1,)), ((), ())), preferred_element_type=F32)


def nn(a, b):
    return lax.dot_general(a, b, (((1,), (0,)), ((), ())), preferred_element_type=F32)


def lanes(shape):
    return lax.broadcasted_iota(jnp.int32, shape, len(shape) - 1)


def subs(shape):
    return lax.broadcasted_iota(jnp.int32, shape, len(shape) - 2)


def split(x):
    hi = x.astype(BF16).astype(F32)
    return hi, x - hi


def send_body(corpus, codes, meta, cent, out, turned, words, rows_s):
    for p in range(4):
        for w in range(6):
            for h in range(2):
                rows_s[h * 64 : (h + 1) * 64, :] = corpus[w, pl.ds(2 * p + h, 64, stride=8), :]
            turned[w * 128 : (w + 1) * 128, :] = rows_s[...].T
        for c in range(6):
            out[pl.ds(p * 8 + c, 128, stride=CH), :] = turned[pl.ds(c, 128, stride=6), :]
        for h in range(2):
            rows_s[h * 64 : (h + 1) * 64, :] = codes[pl.ds(2 * p + h, 64, stride=8), :]
        words[...] = rows_s[...].T
        for j in range(4):
            for k, pick in ((6, FIRST[j]), (7, SECOND[j])):
                out[pl.ds(j * CH + p * 8 + k, 32, stride=4 * CH), :] = words[pl.ds(pick, 32, stride=3), :]
    for k in range(5):
        out[pl.ds(32 + k, 128, stride=CH), :] = jnp.broadcast_to(meta[k : k + 1, :], (128, 128))
    for w in range(6):
        rows_s[...] = jnp.zeros((128, 128), F32)
        rows_s[0:32, :] = cent[:, w * 128 : (w + 1) * 128]
        turned[w * 128 : (w + 1) * 128, :] = rows_s[...].T
    parts = [turned[pl.ds(c, 128, stride=6), :] for c in range(6)]
    for k, cols in ((5, (0, 1, 2, 3)), (6, (4, 5))):
        row = parts[cols[0]]
        for i, c in enumerate(cols[1:], 1):
            row = row + pltpu.roll(parts[c], 32 * i, 1)
        out[pl.ds(32 + k, 128, stride=CH), :] = row
    out[pl.ds(39, 128, stride=CH), :] = jnp.zeros((128, 128), F32)


def row_info(tile):
    lane = lanes((8, 128))
    counts = tile[4:5, :]
    counts = jnp.where(lane[0:1] < 64, pltpu.roll(counts, 64, 1), counts)
    place = 2 * subs((8, 128)) + (lane >= 64).astype(jnp.int32)
    used = place < counts.astype(jnp.int32)
    return tile.astype(jnp.int32), used


GRP_SRC = 4


def sums_body(recv, out, acc):
    acc[...] = jnp.zeros((256, 256), F32)
    sub8 = subs((8, 128))
    digits = subs((256, 128)).astype(F32).astype(BF16)

    def step(i, carry):
        left, right = [], []
        for k in range(GRP_SRC):
            base = pl.multiple_of((i * GRP_SRC + k) * CH, 8)
            label, used = row_info(recv[pl.ds(base + 32, 8), :])
            low = jnp.where(used, label & 255, -1).astype(F32).astype(BF16)
            high = (label >> 8).astype(F32).astype(BF16)
            for p in range(4):
                x = recv[pl.ds(base + 8 * p, 8), :]
                hi, lo = split(x)
                hi = jnp.where(sub8 < 6, hi, jnp.where(sub8 == 6, 1.0, 0.0))
                lo = jnp.where(sub8 < 6, lo, 0.0)
                xb = jnp.concatenate([hi, lo], 0).astype(BF16)
                sel = jnp.broadcast_to(high[p : p + 1, :], (16, 128))
                left.append(
                    jnp.concatenate([jnp.where(sel == jnp.asarray(v, BF16), xb, jnp.zeros_like(xb)) for v in range(16)], 0)
                )
                right.append(jnp.where(digits == jnp.broadcast_to(low[p : p + 1, :], (256, 128)),
                                       jnp.ones((256, 128), BF16), jnp.zeros((256, 128), BF16)))
        acc[...] += nt(jnp.concatenate(left, 1), jnp.concatenate(right, 1))
        return carry

    lax.fori_loop(0, 128 // GRP_SRC, step, 0)

    lane = lanes((8, 128))

    def finish(s, carry):
        sel = s // 2
        old = jnp.zeros((8, 128), F32)
        for g in range(4):
            tile = recv[pl.ds(pl.multiple_of((s * 4 + g) * CH + 32, 8), 8), :]
            both = jnp.where(sub8 < 4, jnp.broadcast_to(tile[5:6, :], (8, 128)), jnp.broadcast_to(tile[6:7, :], (8, 128)))
            moved = jnp.zeros((8, 128), F32)
            for c in range(4):
                moved = jnp.where((sub8 & 3) == c, pltpu.roll(both, (32 * (g - c)) % 128, 1), moved)
            old = jnp.where((lane >> 5) == g, moved, old)
        old = jnp.where(sub8 < 6, old, 0.0)
        rows = acc[pl.ds(pl.multiple_of(sel * 16, 16), 16), :]
        rows = jnp.where((s & 1) == 0, rows[:, :128], rows[:, 128:])
        total = rows[0:8] + rows[8:16]
        count = jnp.broadcast_to(total[6:7, :], (8, 128))
        fresh = (total + PRIOR * old) / (count + PRIOR)
        out[s] = jnp.where(sub8 < 6, fresh, 0.0)
        return carry

    lax.fori_loop(0, 32, finish, 0)


def code_digits(x, first, second_cols, used):
    a = jnp.broadcast_to(x[6:7, :], (8, 128))
    b = jnp.broadcast_to(x[7:8, :], (8, 128))
    return a, b


def resid_body(place, recv, fresh, book, resid, table, shown, left, acc):
    first = place[0]
    sub8 = subs((8, 128))
    lane = lanes((8, 128))
    digits = subs((256, 128)).astype(F32).astype(BF16)
    digit64 = subs((64, 128)).astype(F32).astype(BF16)
    for sel in range(16):
        for h in range(2):
            hi, lo = split(fresh[2 * sel + h])
            left[sel * 16 : (sel + 1) * 16, h * 128 : (h + 1) * 128] = jnp.concatenate([hi, lo], 0).astype(BF16)
    acc[...] = jnp.zeros((64, 128), F32)
    one, zero = jnp.ones((), BF16), jnp.zeros((), BF16)
    is_first = (sub8 < first) | (sub8 == 6)

    def step(i, carry):
        lhs, rhs = [], []
        for k in range(2):
            src = i * 2 + k
            base = pl.multiple_of(src * CH, 8)
            label, used = row_info(recv[pl.ds(base + 32, 8), :])
            low = (label & 255).astype(F32).astype(BF16)
            high = label >> 8
            hot = [jnp.where(digits == jnp.broadcast_to(low[p : p + 1, :], (256, 128)),
                             jnp.ones((256, 128), BF16), jnp.zeros((256, 128), BF16)) for p in range(4)]
            got = nn(left[...], jnp.concatenate(hot, 1))
            for p in range(4):
                x = recv[pl.ds(base + 8 * p, 8), :]
                sel = jnp.broadcast_to(high[p : p + 1, :], (8, 128))
                ghi = jnp.zeros((8, 128), F32)
                glo = jnp.zeros((8, 128), F32)
                for v in range(16):
                    hit = sel == v
                    ghi = jnp.where(hit, got[v * 16 : v * 16 + 8, p * 128 : (p + 1) * 128], ghi)
                    glo = jnp.where(hit, got[v * 16 + 8 : v * 16 + 16, p * 128 : (p + 1) * 128], glo)
                r = x - (ghi + glo)
                resid[src * 4 + p] = r
                a = jnp.broadcast_to(x[6:7, :], (8, 128))
                b = jnp.broadcast_to(x[7:8, :], (8, 128))
                code = jnp.where(is_first, a, b).astype(jnp.int32)
                use = used[p : p + 1, :]
                pick = jnp.where(jnp.broadcast_to(use, (8, 128)), code >> 6, -1).astype(F32)
                pick = jnp.concatenate([pick, pick], 0).astype(BF16)
                hi, lo = split(r)
                hi = jnp.where(sub8 < 6, hi, 1.0)
                lo = jnp.where(sub8 < 6, lo, 0.0)
                rb = jnp.concatenate([hi, lo], 0).astype(BF16)
                lhs.append(jnp.concatenate([jnp.where(pick == jnp.asarray(v, BF16), rb, jnp.zeros_like(rb)) for v in range(4)], 0))
                da = (x[6:7, :].astype(jnp.int32) & 63).astype(F32).astype(BF16)
                db = (x[7:8, :].astype(jnp.int32) & 63).astype(F32).astype(BF16)
                rhs.append(jnp.concatenate(
                    [jnp.where(digit64 == jnp.broadcast_to(d, (64, 128)), jnp.ones((64, 128), BF16), jnp.zeros((64, 128), BF16))
                     for d in (da, db)], 0))
        acc[...] += nt(jnp.concatenate(lhs, 1), jnp.concatenate(rhs, 1))
        return carry

    lax.fori_loop(0, 64, step, 0)

    valid = ((sub8 < first) == (lane < 64)) & (sub8 < 6)
    made = []
    for sel in range(4):
        total = acc[sel * 16 : sel * 16 + 8, :] + acc[sel * 16 + 8 : sel * 16 + 16, :]
        count = jnp.where(lane < 64, jnp.broadcast_to(total[6:7, :], (8, 128)), jnp.broadcast_to(total[7:8, :], (8, 128)))
        new = (total + PRIOR * book[sel]) / (count + PRIOR)
        new = jnp.where(valid, new, 0.0)
        table[sel] = new
        made.append(new + pltpu.roll(new, 64, 1))
    shown[0] = jnp.where(lane < 64, made[0], made[1])
    shown[1] = jnp.where(lane < 64, made[2], made[3])


def error_body(place, recv, resid, table, out, err, mixed, left):
    first = place[0]
    sub8 = subs((8, 128))
    lane = lanes((8, 128))
    digit64 = subs((64, 128)).astype(F32).astype(BF16)
    is_first = sub8 < first
    for sel in range(4):
        hi, lo = split(table[sel])
        left[sel * 16 : (sel + 1) * 16, :] = jnp.concatenate([hi, lo], 0).astype(BF16)

    def look(src, carry):
        base = pl.multiple_of(src * CH, 8)
        unused, used = row_info(recv[pl.ds(base + 32, 8), :])
        hot = []
        for p in range(4):
            r = resid[src * 4 + p]
            da = (r[6:7, :].astype(jnp.int32) & 63).astype(F32).astype(BF16)
            db = (r[7:8, :].astype(jnp.int32) & 63).astype(F32).astype(BF16)
            hot.append(jnp.concatenate(
                [jnp.where(digit64 == jnp.broadcast_to(d, (64, 128)), jnp.ones((64, 128), BF16), jnp.zeros((64, 128), BF16))
                 for d in (da, db)], 0))
        got = nn(left[...], jnp.concatenate(hot, 1))
        for p in range(4):
            r = resid[src * 4 + p]
            a = jnp.broadcast_to(r[6:7, :], (8, 128))
            b = jnp.broadcast_to(r[7:8, :], (8, 128))
            pick = jnp.where(is_first, a, b).astype(jnp.int32) >> 6
            whi = jnp.zeros((8, 128), F32)
            wlo = jnp.zeros((8, 128), F32)
            for v in range(4):
                hit = pick == v
                whi = jnp.where(hit, got[v * 16 : v * 16 + 8, p * 128 : (p + 1) * 128], whi)
                wlo = jnp.where(hit, got[v * 16 + 8 : v * 16 + 16, p * 128 : (p + 1) * 128], wlo)
            e = jnp.where(jnp.broadcast_to(used[p : p + 1, :], (8, 128)) & (sub8 < 6), r - (whi + wlo), 0.0)
            err[src * 4 + p] = e
        return carry

    lax.fori_loop(0, 128, look, 0)

    spots = subs((512, 128))
    spot_lane = lanes((1, 128))

    def group(g, carry):
        def gather(sh, carry2):
            cols, hots = [], []
            for pair in range(2):
                srcs = [sh * 16 + (2 * pair + q) * 4 + g for q in range(2)]
                aims = []
                for q in range(2):
                    row = recv[pl.ds(srcs[q] * CH + 36, 1), :].astype(jnp.int32)
                    aims.append((row >> 2) * 16 + (row & 3) + (2 * pair + q) * 4)
                aim = jnp.where(spot_lane < 64, aims[0], pltpu.roll(aims[1], 64, 1))
                hots.append(jnp.where(spots == jnp.broadcast_to(aim, (512, 128)), 1.0, 0.0).astype(BF16))
                rows = []
                for p in range(4):
                    e0 = err[srcs[0] * 4 + p]
                    e1 = err[srcs[1] * 4 + p]
                    rows.append(jnp.where(lane < 64, e0, pltpu.roll(e1, 64, 1)))
                    rows.append(jnp.where(lane < 64, pltpu.roll(e0, 64, 1), e1))
                cols.append(jnp.concatenate(rows, 0).astype(BF16))
            mixed[sh] = nt(jnp.concatenate(cols, 1), jnp.concatenate(hots, 1))
            return carry2

        lax.fori_loop(0, 8, gather, 0)
        for v in range(4):
            for r in range(8):
                z = [mixed[sh, r * 8 : (r + 1) * 8, v * 128 : (v + 1) * 128] for sh in range(8)]
                for bit in range(3):
                    step = 1 << bit
                    keep = ((lane >> (4 + bit)) & 1) == 0
                    nz = list(z)
                    for i in range(8):
                        if i & step:
                            continue
                        a, b = z[i], z[i | step]
                        nz[i] = jnp.where(keep, a, pltpu.roll(b, 16 * step, 1))
                        nz[i | step] = jnp.where(keep, pltpu.roll(a, 128 - 16 * step, 1), b)
                    z = nz
                for tl in range(8):
                    t = 8 * v + tl
                    out[pl.ds((t * 4 + g) * 48 + r, 6, stride=8), :] = z[tl][0:6, :]
        return carry

    lax.fori_loop(0, 4, group, 0)


def place_body(recv, out, turned):
    for r in range(8):
        for w in range(6):
            turned[w, pl.ds(r, 128, stride=8), :] = recv[pl.ds(w * 1024 + r, 128, stride=8), :].T
    for w in range(6):
        out[:, :, w * 128 : (w + 1) * 128] = turned[w].reshape(128, 8, 128).astype(BF16)


def columns_body(parts, recv, out, turned):
    for h in range(parts):
        for c in range(6):
            turned[pl.ds(c, 128, stride=6), :] = recv[pl.ds(h * 8 + c, 128, stride=8 * parts), :]
        for w in range(6):
            out[h * 128 : (h + 1) * 128, w * 128 : (w + 1) * 128] = turned[w * 128 : (w + 1) * 128, :].T


def slot_ranks(dest):
    count = dest.shape[0]
    order = jnp.arange(count, dtype=jnp.int32)
    same = (dest[:, None] == dest[None, :]) & (order[None, :] < order[:, None])
    return jnp.sum(same.astype(jnp.int32), axis=1)


def local(corpus, block_rows, targets, assign, codes, centroids, codebook):
    grp = lax.axis_index("grp")
    me = lax.axis_index("shard") * 4 + grp
    first = jnp.where(grp == 1, 2, jnp.where(grp == 2, 4, 6)).astype(jnp.int32).reshape(1)
    dest = targets[:, 0]
    slot = dest * 4 + slot_ranks(dest)
    meta = jnp.concatenate(
        [assign.T.reshape(4, 128), jnp.concatenate([slot, block_rows]).reshape(1, 128), jnp.zeros((3, 128), jnp.int32)], 0
    ).astype(F32)
    quarter = lax.dynamic_slice(centroids, (grp * 32, 0), (32, 768))
    rows = corpus.reshape(512, 6, 128).transpose(1, 0, 2)
    words = jnp.pad(codes.reshape(512, 96).astype(F32), ((0, 0), (0, 32)))

    sent = call(
        send_body,
        jax.ShapeDtypeStruct((128 * CH, 128), F32),
        [pltpu.VMEM((768, 128), F32), pltpu.VMEM((128, 128), F32), pltpu.VMEM((128, 128), F32)],
        moved=5 << 20,
    )(rows, words, meta, quarter)
    recv = lax.all_to_all(sent.reshape(128, CH, 128), BOTH, 0, 0, tiled=True).reshape(128 * CH, 128)

    fresh = call(
        sums_body, jax.ShapeDtypeStruct((32, 8, 128), F32), [pltpu.VMEM((256, 256), F32)], flops=1 << 33, moved=3 << 20
    )(recv)
    owned = lax.all_to_all(
        jnp.broadcast_to(fresh[:, None], (32, 4, 8, 128)).reshape(128, 8, 128), BOTH, 0, 0, tiled=True
    )

    old = lax.dynamic_slice(codebook, (0, 6 * me), (256, 6)).T.reshape(6, 4, 64).transpose(1, 0, 2)
    old = jnp.pad(jnp.concatenate([old, old], 2), ((0, 0), (0, 2), (0, 0)))
    smem = pl.BlockSpec(memory_space=pltpu.SMEM)
    vmem = pl.BlockSpec(memory_space=pltpu.VMEM)
    params = pltpu.CompilerParams(vmem_limit_bytes=VMEM_LIMIT)
    resid, table, shown = pl.pallas_call(
        resid_body,
        in_specs=[smem, vmem, vmem, vmem],
        out_shape=(
            jax.ShapeDtypeStruct((512, 8, 128), F32),
            jax.ShapeDtypeStruct((4, 8, 128), F32),
            jax.ShapeDtypeStruct((2, 8, 128), F32),
        ),
        scratch_shapes=[pltpu.VMEM((256, 256), BF16), pltpu.VMEM((64, 128), F32)],
        compiler_params=params,
        cost_estimate=pl.CostEstimate(flops=1 << 33, bytes_accessed=5 << 20, transcendentals=0),
    )(first, recv, fresh, old)
    books = lax.all_to_all(jnp.broadcast_to(shown.reshape(1, 16, 128), (128, 16, 128)), BOTH, 0, 0, tiled=True)

    errors = pl.pallas_call(
        error_body,
        in_specs=[smem, vmem, vmem, vmem],
        out_shape=jax.ShapeDtypeStruct((128 * 48, 128), F32),
        scratch_shapes=[
            pltpu.VMEM((512, 8, 128), F32),
            pltpu.VMEM((8, 64, 512), F32),
            pltpu.VMEM((64, 128), BF16),
        ],
        compiler_params=params,
        cost_estimate=pl.CostEstimate(flops=1 << 32, bytes_accessed=8 << 20, transcendentals=0),
    )(first, recv, resid, table)
    landed = lax.all_to_all(errors.reshape(128, 48, 128), BOTH, 0, 0, tiled=True).reshape(128 * 48, 128)

    turned = [pltpu.VMEM((768, 128), F32)]
    new_centroids = call(
        lambda *refs: columns_body(1, *refs), jax.ShapeDtypeStruct((128, 768), F32), turned, moved=1 << 20
    )(owned.reshape(1024, 128))
    new_codebook = call(
        lambda *refs: columns_body(2, *refs), jax.ShapeDtypeStruct((256, 768), F32), turned, moved=2 << 20
    )(books.reshape(2048, 128))
    moved_error = call(
        place_body, jax.ShapeDtypeStruct((128, 8, 768), BF16), [pltpu.VMEM((6, 1024, 128), F32)], moved=5 << 20
    )(landed)
    return (new_centroids, moved_error, new_codebook)


def solution(mesh):
    in_specs = (
        P(BOTH, None, None),
        P(BOTH),
        P(BOTH, None),
        P(BOTH, None),
        P(BOTH, None, None),
        P("shard", None),
        P(),
    )
    out_specs = (P("shard", None), P(BOTH, None, None), P())
    return jax.shard_map(local, mesh=mesh, in_specs=in_specs, out_specs=out_specs, check_vma=False)
```

time: 880 us -> 241 us (0.27)
  waiting for transfers between devices: 338 us -> 73.1 us
  local copies, waits for them, and re-layouts: 175 us -> 11.6 us
  blocking collectives: 130 us -> 0 us
  matrix products: 119 us -> 0 us
  Pallas kernels: 0 us -> 118 us
  other arithmetic: 68 us -> 1.63 us
  between operations: 14.7 us -> 0.78 us
    psum x2 -> x0, waiting for transfers between devices: 145 us -> none  [the longest x1 145 us: local(): lax.psum((csum.reshape(subs, books * sub_width), ccount), ('shard', 'grp'))]
    unnamed x1 -> x0, blocking collectives: 121 us -> none
    dot_general x8 -> x0, matrix products: 119 us -> none  [the longest x4 64.5 us: add_group(): jnp.einsum('rmc,rms->mcs', table, piece, precision=lax.Precision.HIGHEST)]
    pallas_call x0 -> x7, Pallas kernels: none -> 118 us  [the longest x1 49.4 us: local(): pl.pallas_call(error_body, in_specs=[smem, vmem, vmem, vmem], out_shape=j...]
    reduce_scatter x1 -> x0, waiting for transfers between devices: 102 us -> none  [local(): lax.psum_scatter(sums, 'shard', scatter_dimension=0, tiled=True)]
    reshape x2 -> x4, local copies, waits for them, and re-layouts: 66.2 us -> 3.16 us  [the longest x2 2.99 us: local(): rows = corpus.reshape(512, 6, 128).transpose(1, 0, 2)]
    while x2 -> x0, local copies, waits for them, and re-layouts: 39.5 us -> none  [look_up_words(): picked = lax.map(pick, word_groups)]
    unnamed x33 -> x16, local copies, waits for them, and re-layouts: 39.9 us -> 2.53 us
  transfers between devices with their start and end apart: 8 -> 4, of which waited for: 6 -> 2; matrix products, arithmetic and copies ran while one was open for 3% -> 0% of each run, Pallas kernels for 0% -> 36%
where the time goes in v1:
time: 241 us; the launch traced here: 240 us
  Pallas kernels  118 us (49%)
  waiting for transfers between devices  73.1 us (30%)
  starting transfers between devices  35.2 us (15%)
  local copies, waits for them, and re-layouts  11.6 us (5%)
    pallas_call x1, Pallas kernels, local(): pl.pallas_call(error_body, in_specs=[smem, vmem, vmem, vmem], out_shape=j...  49.4 us
    all_to_all x1, waiting for transfers between devices, local(): lax.all_to_all(errors.reshape(128, 48, 128), BOTH, 0, 0, tiled=True)  37.4 us
    all_to_all x1, waiting for transfers between devices, local(): lax.all_to_all(sent.reshape(128, CH, 128), BOTH, 0, 0, tiled=True)  35.7 us
    pallas_call x1, Pallas kernels, local(): pl.pallas_call(resid_body, in_specs=[smem, vmem, vmem, vmem], out_shape=(...  32.7 us
    pallas_call x1, Pallas kernels, local(): call(sums_body, jax.ShapeDtypeStruct((32, 8, 128), F32), [pltpu.VMEM((256...  23.1 us
    all_to_all x1, starting transfers between devices, local(): lax.all_to_all(sent.reshape(128, CH, 128), BOTH, 0, 0, tiled=True)  11.5 us
    all_to_all x1, starting transfers between devices, local(): lax.all_to_all(errors.reshape(128, 48, 128), BOTH, 0, 0, tiled=True)  10.2 us
    all_to_all x1, starting transfers between devices, local(): lax.all_to_all(jnp.broadcast_to(shown.reshape(1, 16, 128), (128, 16, 128)...  9.9 us
  transfers between devices with their start and end apart: 4, of which 2 were waited for; matrix products, arithmetic and copies ran while one was open for 0% of the time, Pallas kernels for 36%

profile of v1, /device:TPU:1, one launch (start us, length us, event | category | flops | bytes accessed | tf_op | source)
XLA Modules:
  0.0 240.2 jit_solution(3260526191087435964)
XLA Ops:
  0.6 0.0 copy-start
  0.7 1.6 reshape.48
  2.2 0.0 copy-start.5
  2.2 0.0 copy-start.6
  2.3 1.4 copy.19
  3.7 0.1 reshape.49
  3.8 0.2 convert_reduce_fusion
  4.0 0.1 pad.14.clone
  4.1 1.5 constant_dynamic-slice_fusion.1.cent
  5.6 0.7 pad.8.codes
  6.3 0.1 add_bitcast_fusion
  6.4 0.7 add_convert_fusion.meta
  7.1 4.1 %shard_map.94 = f32[5120,128]{1,0:T(8,128)} custom-call(f32[6,512,128]{2,1,0:T(8,128)} %bitcast.24, f32[512,128]{1,0:T(8,128)} %pad.8.codes, f32[8,128]{1,0:T(8,128)} %add_convert_fusion.meta, f32[32,768]{1,0:T(8,128)} %constant_dynamic-slice_fusion.1.cent), custom_call_target="tpu_custom_call" | custom-call | bytes 5242880 | tf_op jit(solution)/shard_map/pallas_call | solution.py:342
  11.2 11.5 %all-to-all-start = ((f32[128,40,128]{2,1,0:T(8,128)}), f32[128,40,128]{2,1,0:T(8,128)S(1)}, u32[]{:S(2)}, u32[]{:S(2)}) async-start(f32[128,40,128]{2,1,0:T(8,128)} %bitcast.23), calls=%async_computation | async-start | bytes 5242880 | tf_op jit(solution)/shard_map/all_to_all | solution.py:348
  22.7 0.1 constant_dynamic-slice_fusion
  22.8 0.1 copy.15
  22.9 0.7 select_maximum_fusion.book
  23.6 35.7 %all-to-all-done = f32[128,40,128]{2,1,0:T(8,128)S(1)} async-done(((f32[128,40,128]{2,1,0:T(8,128)}), f32[128,40,128]{2,1,0:T(8,128)S(1)}, u32[]{:S(2)}, u32[]{:S(2)}) %all-to-all-start) | async-done | bytes 2621472 | tf_op jit(solution)/shard_map/all_to_all | solution.py:348
  59.3 1.5 copy-done.2
  60.9 23.1 %shard_map.95.fresh = f32[32,8,128]{2,1,0:T(8,128)} custom-call(f32[5120,128]{1,0:T(8,128)} %bitcast.27), custom_call_target="tpu_custom_call" | custom-call | flops 8589934592 | bytes 3145728 | tf_op jit(solution)/shard_map/pallas_call | solution.py:350
  83.9 1.7 broadcast_in_dim.9
  85.7 3.7 %all-to-all-start.1 = ((f32[128,8,128]{2,1,0:T(8,128)}), f32[128,8,128]{2,1,0:T(8,128)S(1)}, u32[]{:S(2)}, u32[]{:S(2)}) async-start(f32[128,8,128]{2,1,0:T(8,128)} %bitcast.7), calls=%async_computation.1 | async-start | bytes 1048576 | tf_op jit(solution)/shard_map/all_to_all | solution.py:353
  89.3 32.7 %shard_map.97 = (f32[512,8,128]{2,1,0:T(8,128)}, f32[4,8,128]{2,1,0:T(8,128)}, f32[2,8,128]{2,1,0:T(8,128)}) custom-call(s32[1]{0:T(128)} %bitcast.9.place, f32[5120,128]{1,0:T(8,128)} %bitcast.28, f32[32,8,128]{2,1,0:T(8,128)} %shard_map.95.fresh, f32[4,8,128]{2,1,0:T(8,128)} %select_maximum_fusion.book), custom_call_target="tpu_custom_call" | custom-call | flops 8589934592 | bytes 5242880 | tf_op jit(solution)/shard_map/pallas_call | solution.py:362
  122.0 1.7 broadcast_in_dim.21
  123.8 9.9 %all-to-all-start.3 = ((f32[128,16,128]{2,1,0:T(8,128)}), f32[128,16,128]{2,1,0:T(8,128)S(1)}, u32[]{:S(2)}, u32[]{:S(2)}) async-start(f32[128,16,128]{2,1,0:T(8,128)} %broadcast_in_dim.21), calls=%async_computation.3 | async-start | bytes 2097152 | tf_op jit(solution)/shard_map/all_to_all | solution.py:374
  133.7 49.4 %shard_map.98 = f32[6144,128]{1,0:T(8,128)} custom-call(s32[1]{0:T(128)} %bitcast.9.place, f32[5120,128]{1,0:T(8,128)} %bitcast.29, f32[512,8,128]{2,1,0:T(8,128)} %get-tuple-element.6.resid, f32[4,8,128]{2,1,0:T(8,128)} %get-tuple-element.7.table), custom_call_target="tpu_custom_call" | custom-call | flops 4294967296 | bytes 8388608 | tf_op jit(solution)/shard_map/pallas_call | solution.py:376
  183.1 1.0 copy-done.1
  184.1 10.2 %all-to-all-start.2 = ((f32[128,48,128]{2,1,0:T(8,128)}), f32[128,48,128]{2,1,0:T(8,128)}, u32[]{:S(2)}, u32[]{:S(2)}) async-start(f32[128,48,128]{2,1,0:T(8,128)} %bitcast.26), calls=%async_computation.2 | async-start | bytes 6291456 | tf_op jit(solution)/shard_map/all_to_all | solution.py:388
  194.2 2.0 shard_map.96
  196.2 2.5 %shard_map.100 = f32[256,768]{1,0:T(8,128)} custom-call(f32[2048,128]{1,0:T(8,128)} %bitcast.25), custom_call_target="tpu_custom_call" | custom-call | bytes 2097152 | tf_op jit(solution)/shard_map/pallas_call | solution.py:394
  198.8 37.4 %all-to-all-done.2 = f32[128,48,128]{2,1,0:T(8,128)} async-done(((f32[128,48,128]{2,1,0:T(8,128)}), f32[128,48,128]{2,1,0:T(8,128)}, u32[]{:S(2)}, u32[]{:S(2)}) %all-to-all-start.2) | async-done | bytes 3145760 | tf_op jit(solution)/shard_map/all_to_all | solution.py:388
  236.2 4.1 %shard_map.99 = bf16[128,8,768]{2,1,0:T(8,128)(2,1)} custom-call(f32[6144,128]{1,0:T(8,128)} %bitcast.14.recv), custom_call_target="tpu_custom_call" | custom-call | bytes 5242880 | tf_op jit(solution)/shard_map/pallas_call | solution.py:397
  (16 shorter events, 0.1 us)
Async XLA Ops:
  0.6 22.1 %copy-start = (f32[256,768]{1,0:T(8,128)S(1)}, f32[256,768]{1,0:T(8,128)}, u32[]{:S(2)}) copy-start(f32[256,768]{1,0:T(8,128)} %param.13) | copy-start | bytes 2359300
  2.2 1.5 copy-start.4
  2.2 1.5 copy-start.5
  2.2 1.6 copy-start.6
  2.3 4.1 %copy-start.7 = (s32[64]{0:T(128)S(1)}, s32[64]{0:T(128)}, u32[]{:S(2)}) copy-start(s32[64]{0:T(128)} %param.8) | copy-start | bytes 772
  11.2 48.1 %all-to-all-start = ((f32[128,40,128]{2,1,0:T(8,128)}), f32[128,40,128]{2,1,0:T(8,128)S(1)}, u32[]{:S(2)}, u32[]{:S(2)}) async-start(f32[128,40,128]{2,1,0:T(8,128)} %bitcast.23), calls=%async_computation | async-start | bytes 5242880 | tf_op jit(solution)/shard_map/all_to_all | solution.py:348
  59.3 1.5 copy-start.2
  85.7 36.4 %all-to-all-start.1 = ((f32[128,8,128]{2,1,0:T(8,128)}), f32[128,8,128]{2,1,0:T(8,128)S(1)}, u32[]{:S(2)}, u32[]{:S(2)}) async-start(f32[128,8,128]{2,1,0:T(8,128)} %bitcast.7), calls=%async_computation.1 | async-start | bytes 1048576 | tf_op jit(solution)/shard_map/all_to_all | solution.py:353
  122.0 61.0 %copy-start.3 = (f32[128,8,128]{2,1,0:T(8,128)}, f32[128,8,128]{2,1,0:T(8,128)S(1)}, u32[]{:S(2)}) copy-start(f32[128,8,128]{2,1,0:T(8,128)S(1)} %all-to-all-done.1) | copy-start | bytes 1572868
  123.8 59.3 %all-to-all-start.3 = ((f32[128,16,128]{2,1,0:T(8,128)}), f32[128,16,128]{2,1,0:T(8,128)S(1)}, u32[]{:S(2)}, u32[]{:S(2)}) async-start(f32[128,16,128]{2,1,0:T(8,128)} %broadcast_in_dim.21), calls=%async_computation.3 | async-start | bytes 2097152 | tf_op jit(solution)/shard_map/all_to_all | solution.py:374
  183.1 1.0 copy-start.1
  184.1 52.1 %all-to-all-start.2 = ((f32[128,48,128]{2,1,0:T(8,128)}), f32[128,48,128]{2,1,0:T(8,128)}, u32[]{:S(2)}, u32[]{:S(2)}) async-start(f32[128,48,128]{2,1,0:T(8,128)} %bitcast.26), calls=%async_computation.2 | async-start | bytes 6291456 | tf_op jit(solution)/shard_map/all_to_all | solution.py:388

commit v2 on v1

v2 whole, which is shorter than its diff:
```python
import jax
import jax.numpy as jnp
from jax import lax
from jax.experimental import pallas as pl
from jax.experimental.pallas import tpu as pltpu
from jax.sharding import PartitionSpec as P

PRIOR = 8.0
BOTH = ("shard", "grp")
F32 = jnp.float32
BF16 = jnp.bfloat16

CH = 40
FIRST = (0, 0, 1, 2)
SECOND = (0, 1, 2, 2)


def call(body, out, scratch, mib, scalar=False, operands=1, flops=0, moved=0):
    vmem = pl.BlockSpec(memory_space=pltpu.VMEM)
    return pl.pallas_call(
        body,
        in_specs=([pl.BlockSpec(memory_space=pltpu.SMEM)] if scalar else []) + [vmem] * operands,
        out_shape=out,
        scratch_shapes=list(scratch),
        compiler_params=pltpu.CompilerParams(vmem_limit_bytes=mib << 20),
        cost_estimate=pl.CostEstimate(flops=flops, bytes_accessed=moved, transcendentals=0),
    )


def nt(a, b):
    return lax.dot_general(a, b, (((1,), (1,)), ((), ())), preferred_element_type=F32)


def nn(a, b):
    return lax.dot_general(a, b, (((1,), (0,)), ((), ())), preferred_element_type=F32)


def lanes(shape):
    return lax.broadcasted_iota(jnp.int32, shape, len(shape) - 1)


def subs(shape):
    return lax.broadcasted_iota(jnp.int32, shape, len(shape) - 2)


def split(x):
    hi = x.astype(BF16).astype(F32)
    return hi, x - hi


def send_body(place, corpus, codes, meta, cent, out, turned, words, rows_s, codes_s, rows_c):
    codes_s[:, 0:96] = codes[...].astype(F32)
    for w in range(6):
        rows_c[w] = corpus[:, w * 128 : (w + 1) * 128]
    for p in range(4):
        for w in range(6):
            for h in range(2):
                rows_s[h * 64 : (h + 1) * 64, :] = rows_c[w, pl.ds(2 * p + h, 64, stride=8), :]
            turned[w * 128 : (w + 1) * 128, :] = rows_s[...].T
        for c in range(6):
            out[pl.ds(p * 8 + c, 128, stride=CH), :] = turned[pl.ds(c, 128, stride=6), :]
        for h in range(2):
            rows_s[h * 64 : (h + 1) * 64, :] = codes_s[pl.ds(2 * p + h, 64, stride=8), :]
        words[...] = rows_s[...].T
        for j in range(4):
            for k, pick in ((6, FIRST[j]), (7, SECOND[j])):
                out[pl.ds(j * CH + p * 8 + k, 32, stride=4 * CH), :] = words[pl.ds(pick, 32, stride=3), :]
    for k in range(5):
        out[pl.ds(32 + k, 128, stride=CH), :] = jnp.broadcast_to(meta[k : k + 1, :], (128, 128))
    start = pl.multiple_of(place[1] * 32, 32)
    for w in range(6):
        rows_s[0:32, :] = cent[pl.ds(start, 32), w * 128 : (w + 1) * 128]
        rows_s[32:128, :] = jnp.zeros((96, 128), F32)
        turned[w * 128 : (w + 1) * 128, :] = rows_s[...].T
    parts = [turned[pl.ds(c, 128, stride=6), :] for c in range(6)]
    for k, cols in ((5, (0, 1, 2, 3)), (6, (4, 5))):
        row = parts[cols[0]]
        for i, c in enumerate(cols[1:], 1):
            row = row + pltpu.roll(parts[c], 32 * i, 1)
        out[pl.ds(32 + k, 128, stride=CH), :] = row
    out[pl.ds(39, 128, stride=CH), :] = jnp.zeros((128, 128), F32)


def row_info(tile):
    lane = lanes((8, 128))
    counts = tile[4:5, :]
    counts = jnp.where(lane[0:1] < 64, pltpu.roll(counts, 64, 1), counts)
    place = 2 * subs((8, 128)) + (lane >= 64).astype(jnp.int32)
    used = place < counts.astype(jnp.int32)
    return tile.astype(jnp.int32), used


GRP_SRC = 32
RES_SRC = 16
LOOK_SRC = 8


def sums_body(recv, out, acc):
    acc[...] = jnp.zeros((256, 256), F32)
    sub8 = subs((8, 128))
    digits = subs((256, 128)).astype(F32).astype(BF16)

    def step(i, carry):
        left, right = [], []
        for k in range(GRP_SRC):
            base = pl.multiple_of((i * GRP_SRC + k) * CH, 8)
            label, used = row_info(recv[pl.ds(base + 32, 8), :])
            low = jnp.where(used, label & 255, -1).astype(F32).astype(BF16)
            high = (label >> 8).astype(F32).astype(BF16)
            for p in range(4):
                x = recv[pl.ds(base + 8 * p, 8), :]
                hi, lo = split(x)
                hi = jnp.where(sub8 < 6, hi, jnp.where(sub8 == 6, 1.0, 0.0))
                lo = jnp.where(sub8 < 6, lo, 0.0)
                xb = jnp.concatenate([hi, lo], 0).astype(BF16)
                sel = jnp.broadcast_to(high[p : p + 1, :], (16, 128))
                left.append(
                    jnp.concatenate([jnp.where(sel == jnp.asarray(v, BF16), xb, jnp.zeros_like(xb)) for v in range(16)], 0)
                )
                right.append(jnp.where(digits == jnp.broadcast_to(low[p : p + 1, :], (256, 128)),
                                       jnp.ones((256, 128), BF16), jnp.zeros((256, 128), BF16)))
        acc[...] += nt(jnp.concatenate(left, 1), jnp.concatenate(right, 1))
        return carry

    lax.fori_loop(0, 128 // GRP_SRC, step, 0)

    lane = lanes((8, 128))

    def finish(s, carry):
        sel = s // 2
        old = jnp.zeros((8, 128), F32)
        for g in range(4):
            tile = recv[pl.ds(pl.multiple_of((s * 4 + g) * CH + 32, 8), 8), :]
            both = jnp.where(sub8 < 4, jnp.broadcast_to(tile[5:6, :], (8, 128)), jnp.broadcast_to(tile[6:7, :], (8, 128)))
            moved = jnp.zeros((8, 128), F32)
            for c in range(4):
                moved = jnp.where((sub8 & 3) == c, pltpu.roll(both, (32 * (g - c)) % 128, 1), moved)
            old = jnp.where((lane >> 5) == g, moved, old)
        old = jnp.where(sub8 < 6, old, 0.0)
        rows = acc[pl.ds(pl.multiple_of(sel * 16, 16), 16), :]
        rows = jnp.where((s & 1) == 0, rows[:, :128], rows[:, 128:])
        total = rows[0:8] + rows[8:16]
        count = jnp.broadcast_to(total[6:7, :], (8, 128))
        fresh = (total + PRIOR * old) / (count + PRIOR)
        out[s] = jnp.where(sub8 < 6, fresh, 0.0)
        return carry

    lax.fori_loop(0, 32, finish, 0)


def code_digits(x, first, second_cols, used):
    a = jnp.broadcast_to(x[6:7, :], (8, 128))
    b = jnp.broadcast_to(x[7:8, :], (8, 128))
    return a, b


def resid_body(place, recv, fresh, book, resid, table, share, left, acc):
    first = place[0]
    sub8 = subs((8, 128))
    lane = lanes((8, 128))
    digits = subs((256, 128)).astype(F32).astype(BF16)
    digit64 = subs((64, 128)).astype(F32).astype(BF16)
    for sel in range(16):
        for h in range(2):
            hi, lo = split(fresh[2 * sel + h])
            left[sel * 16 : (sel + 1) * 16, h * 128 : (h + 1) * 128] = jnp.concatenate([hi, lo], 0).astype(BF16)
    acc[...] = jnp.zeros((64, 128), F32)
    one, zero = jnp.ones((), BF16), jnp.zeros((), BF16)
    is_first = (sub8 < first) | (sub8 == 6)

    def step(i, carry):
        lhs, rhs = [], []
        for k in range(RES_SRC):
            src = i * RES_SRC + k
            base = pl.multiple_of(src * CH, 8)
            label, used = row_info(recv[pl.ds(base + 32, 8), :])
            low = (label & 255).astype(F32).astype(BF16)
            high = label >> 8
            hot = [jnp.where(digits == jnp.broadcast_to(low[p : p + 1, :], (256, 128)),
                             jnp.ones((256, 128), BF16), jnp.zeros((256, 128), BF16)) for p in range(4)]
            got = nn(left[...], jnp.concatenate(hot, 1))
            for p in range(4):
                x = recv[pl.ds(base + 8 * p, 8), :]
                sel = jnp.broadcast_to(high[p : p + 1, :], (8, 128))
                ghi = jnp.zeros((8, 128), F32)
                glo = jnp.zeros((8, 128), F32)
                for v in range(16):
                    hit = sel == v
                    ghi = jnp.where(hit, got[v * 16 : v * 16 + 8, p * 128 : (p + 1) * 128], ghi)
                    glo = jnp.where(hit, got[v * 16 + 8 : v * 16 + 16, p * 128 : (p + 1) * 128], glo)
                r = x - (ghi + glo)
                resid[src * 4 + p] = r
                a = jnp.broadcast_to(x[6:7, :], (8, 128))
                b = jnp.broadcast_to(x[7:8, :], (8, 128))
                code = jnp.where(is_first, a, b).astype(jnp.int32)
                use = used[p : p + 1, :]
                pick = jnp.where(jnp.broadcast_to(use, (8, 128)), code >> 6, -1).astype(F32)
                pick = jnp.concatenate([pick, pick], 0).astype(BF16)
                hi, lo = split(r)
                hi = jnp.where(sub8 < 6, hi, 1.0)
                lo = jnp.where(sub8 < 6, lo, 0.0)
                rb = jnp.concatenate([hi, lo], 0).astype(BF16)
                lhs.append(jnp.concatenate([jnp.where(pick == jnp.asarray(v, BF16), rb, jnp.zeros_like(rb)) for v in range(4)], 0))
                da = (x[6:7, :].astype(jnp.int32) & 63).astype(F32).astype(BF16)
                db = (x[7:8, :].astype(jnp.int32) & 63).astype(F32).astype(BF16)
                rhs.append(jnp.concatenate(
                    [jnp.where(digit64 == jnp.broadcast_to(d, (64, 128)), jnp.ones((64, 128), BF16), jnp.zeros((64, 128), BF16))
                     for d in (da, db)], 0))
        acc[...] += nt(jnp.concatenate(lhs, 1), jnp.concatenate(rhs, 1))
        return carry

    lax.fori_loop(0, 128 // RES_SRC, step, 0)

    valid = ((sub8 < first) == (lane < 64)) & (sub8 < 6)
    made = []
    for sel in range(4):
        total = acc[sel * 16 : sel * 16 + 8, :] + acc[sel * 16 + 8 : sel * 16 + 16, :]
        count = jnp.where(lane < 64, jnp.broadcast_to(total[6:7, :], (8, 128)), jnp.broadcast_to(total[7:8, :], (8, 128)))
        new = (total + PRIOR * book[sel]) / (count + PRIOR)
        new = jnp.where(valid, new, 0.0)
        table[sel] = new
        made.append(new + pltpu.roll(new, 64, 1))
    shown = [jnp.where(lane < 64, made[0], made[1]), jnp.where(lane < 64, made[2], made[3])]

    def spread(s, carry):
        for g in range(4):
            share[s * 4 + g, 0:8, :] = fresh[s]
            share[s * 4 + g, 8:16, :] = shown[0]
            share[s * 4 + g, 16:24, :] = shown[1]
        return carry

    lax.fori_loop(0, 32, spread, 0)


def error_body(place, recv, resid, table, out, left, spread, mixed):
    first = place[0]
    sub8 = subs((8, 128))
    lane = lanes((8, 128))
    digit64 = subs((64, 128)).astype(F32).astype(BF16)
    is_first = sub8 < first
    for sel in range(4):
        hi, lo = split(table[sel])
        left[sel * 16 : (sel + 1) * 16, :] = jnp.concatenate([hi, lo], 0).astype(BF16)
    spread[...] = jnp.zeros(spread.shape, BF16)

    def look(i, carry):
        hot, useds = [], []
        for k in range(8):
            src = i * 8 + k
            base = pl.multiple_of(src * CH, 8)
            unused, used = row_info(recv[pl.ds(base + 32, 8), :])
            useds.append(used)
            for p in range(4):
                r = resid[src * 4 + p]
                da = (r[6:7, :].astype(jnp.int32) & 63).astype(F32).astype(BF16)
                db = (r[7:8, :].astype(jnp.int32) & 63).astype(F32).astype(BF16)
                hot.append(jnp.concatenate(
                    [jnp.where(digit64 == jnp.broadcast_to(d, (64, 128)), jnp.ones((64, 128), BF16), jnp.zeros((64, 128), BF16))
                     for d in (da, db)], 0))
        got = nn(left[...], jnp.concatenate(hot, 1))
        errs = []
        for k in range(8):
            src = i * 8 + k
            for p in range(4):
                q = (k * 4 + p) * 128
                r = resid[src * 4 + p]
                a = jnp.broadcast_to(r[6:7, :], (8, 128))
                b = jnp.broadcast_to(r[7:8, :], (8, 128))
                pick = jnp.where(is_first, a, b).astype(jnp.int32) >> 6
                whi = jnp.zeros((8, 128), F32)
                wlo = jnp.zeros((8, 128), F32)
                for v in range(4):
                    hit = pick == v
                    whi = jnp.where(hit, got[v * 16 : v * 16 + 8, q : q + 128], whi)
                    wlo = jnp.where(hit, got[v * 16 + 8 : v * 16 + 16, q : q + 128], wlo)
                errs.append(jnp.where(jnp.broadcast_to(useds[k][p : p + 1, :], (8, 128)) & (sub8 < 6), r - (whi + wlo), 0.0))
        for g in range(4):
            rows = []
            for p in range(4):
                e0, e1 = errs[g * 4 + p], errs[(g + 4) * 4 + p]
                rows.append(jnp.where(lane < 64, e0, pltpu.roll(e1, 64, 1)))
                rows.append(jnp.where(lane < 64, pltpu.roll(e0, 64, 1), e1))
            spread[i, g * 64 : (g + 1) * 64, g * 128 : (g + 1) * 128] = jnp.concatenate(rows, 0).astype(BF16)
        return carry

    lax.fori_loop(0, 16, look, 0)

    spots = subs((256, 128)).astype(F32).astype(BF16)
    spot_lane = lanes((1, 128))

    def mix(sh, carry):
        total = jnp.zeros((512, 256), F32)
        hots, errs = [], []
        for pair in range(2):
            cols = []
            for g in range(4):
                aims = []
                for q in range(2):
                    src = sh * 16 + (2 * pair + q) * 4 + g
                    row = recv[pl.ds(src * CH + 36, 1), :].astype(jnp.int32)
                    aims.append((row >> 2) * 16 + (row & 3) + (2 * pair + q) * 4)
                aim = jnp.where(spot_lane < 64, aims[0], pltpu.roll(aims[1], 64, 1))
                halves = []
                for h in range(2):
                    at = jnp.broadcast_to((aim - 256 * h).astype(F32).astype(BF16), (256, 128))
                    halves.append(jnp.where(spots == at, jnp.ones((256, 128), BF16), jnp.zeros((256, 128), BF16)))
                cols.append(jnp.concatenate(halves, 0))
            hots.append(jnp.concatenate(cols, 1))
            errs.append(spread[sh * 2 + pair])
        got = nt(jnp.concatenate(hots, 1), jnp.concatenate(errs, 1))
        mixed[:, pl.ds(sh * 16, 16), :] = got.reshape(32, 16, 256)
        return carry

    lax.fori_loop(0, 8, mix, 0)

    def finish(t, carry):
        for h in range(2):
            tile = mixed[t, :, h * 128 : (h + 1) * 128].T
            for g2 in range(2):
                for r in range(8):
                    out[pl.ds((t * 4 + 2 * h + g2) * 48 + r, 6, stride=8), :] = tile[g2 * 64 + r * 8 : g2 * 64 + r * 8 + 6, :]
        return carry

    lax.fori_loop(0, 32, finish, 0)


def place_body(recv, out, turned):
    for r in range(8):
        for w in range(6):
            turned[w, pl.ds(r, 128, stride=8), :] = recv[pl.ds(w * 1024 + r, 128, stride=8), :].T
    for w in range(6):
        out[:, :, w * 128 : (w + 1) * 128] = turned[w].reshape(128, 8, 128).astype(BF16)


def columns_body(recv, centroids, book, turned):
    for h in range(3):
        for c in range(6):
            turned[pl.ds(c, 128, stride=6), :] = recv[pl.ds(h * 8 + c, 128, stride=24), :]
        for w in range(6):
            tile = turned[w * 128 : (w + 1) * 128, :].T
            if h == 0:
                centroids[:, w * 128 : (w + 1) * 128] = tile
            else:
                book[(h - 1) * 128 : h * 128, w * 128 : (w + 1) * 128] = tile


def slot_ranks(dest):
    count = dest.shape[0]
    order = jnp.arange(count, dtype=jnp.int32)
    same = (dest[:, None] == dest[None, :]) & (order[None, :] < order[:, None])
    return jnp.sum(same.astype(jnp.int32), axis=1)


def local(corpus, block_rows, targets, assign, codes, centroids, codebook):
    grp = lax.axis_index("grp")
    me = lax.axis_index("shard") * 4 + grp
    first = jnp.where(grp == 1, 2, jnp.where(grp == 2, 4, 6)).astype(jnp.int32)
    dest = targets[:, 0]
    slot = dest * 4 + slot_ranks(dest)
    meta = jnp.concatenate(
        [assign.T.reshape(4, 128), jnp.concatenate([slot, block_rows]).reshape(1, 128), jnp.zeros((3, 128), jnp.int32)], 0
    ).astype(F32)
    place = jnp.stack([first, grp])

    sent = call(
        send_body,
        jax.ShapeDtypeStruct((128 * CH, 128), F32),
        [pltpu.VMEM((768, 128), F32), pltpu.VMEM((128, 128), F32), pltpu.VMEM((128, 128), F32), pltpu.VMEM((512, 128), F32),
         pltpu.VMEM((6, 512, 128), F32)],
        16,
        scalar=True,
        operands=4,
        moved=5 << 20,
    )(place, corpus.reshape(512, 768), codes.reshape(512, 96), meta, centroids)
    recv = lax.all_to_all(sent.reshape(128, CH, 128), BOTH, 0, 0, tiled=True).reshape(128 * CH, 128)

    fresh = call(
        sums_body,
        jax.ShapeDtypeStruct((32, 8, 128), F32),
        [pltpu.VMEM((256, 256), F32)],
        12,
        flops=1 << 33,
        moved=3 << 20,
    )(recv)

    old = lax.dynamic_slice(codebook, (0, 6 * me), (256, 6)).T.reshape(6, 4, 64).transpose(1, 0, 2)
    old = jnp.pad(jnp.concatenate([old, old], 2), ((0, 0), (0, 2), (0, 0)))
    resid, table, share = call(
        resid_body,
        (
            jax.ShapeDtypeStruct((512, 8, 128), F32),
            jax.ShapeDtypeStruct((4, 8, 128), F32),
            jax.ShapeDtypeStruct((128, 24, 128), F32),
        ),
        [pltpu.VMEM((256, 256), BF16), pltpu.VMEM((64, 128), F32)],
        16,
        scalar=True,
        operands=3,
        flops=1 << 33,
        moved=6 << 20,
    )(place, recv, fresh, old)
    shared = lax.all_to_all(share, BOTH, 0, 0, tiled=True).reshape(128 * 24, 128)

    errors = call(
        error_body,
        jax.ShapeDtypeStruct((128 * 48, 128), F32),
        [pltpu.VMEM((64, 128), BF16), pltpu.VMEM((16, 256, 512), BF16), pltpu.VMEM((32, 128, 256), F32)],
        24,
        scalar=True,
        operands=3,
        flops=1 << 33,
        moved=8 << 20,
    )(place, recv, resid, table)
    landed = lax.all_to_all(errors.reshape(128, 48, 128), BOTH, 0, 0, tiled=True).reshape(128 * 48, 128)

    new_centroids, new_codebook = call(
        columns_body,
        (jax.ShapeDtypeStruct((128, 768), F32), jax.ShapeDtypeStruct((256, 768), F32)),
        [pltpu.VMEM((768, 128), F32)],
        12,
        moved=3 << 20,
    )(shared)
    moved_error = call(
        place_body, jax.ShapeDtypeStruct((128, 8, 768), BF16), [pltpu.VMEM((6, 1024, 128), F32)], 16, moved=5 << 20
    )(landed)
    return (new_centroids, moved_error, new_codebook)


def solution(mesh):
    in_specs = (
        P(BOTH, None, None),
        P(BOTH),
        P(BOTH, None),
        P(BOTH, None),
        P(BOTH, None, None),
        P("shard", None),
        P(),
    )
    out_specs = (P("shard", None), P(BOTH, None, None), P())
    return jax.shard_map(local, mesh=mesh, in_specs=in_specs, out_specs=out_specs, check_vma=False)
```

time: 241 us -> 171 us (0.71)
  Pallas kernels: 118 us -> 52.1 us
  starting transfers between devices: 35.2 us -> 19.9 us
  waiting for transfers between devices: 73.1 us -> 81.9 us
    pallas_call x4 -> x3, Pallas kernels: 86.6 us -> 32.2 us  [the longest x1 16.7 us: local(): call(resid_body, (jax.ShapeDtypeStruct((512, 8, 128), F32), jax.ShapeDtyp...]
    pallas_call x1, Pallas kernels: 23.1 us -> 12.6 us  [local(): call(sums_body, jax.ShapeDtypeStruct((32, 8, 128), F32), [pltpu.VMEM((256...]
    all_to_all x2 -> x1, starting transfers between devices: 13.5 us -> 3.66 us  [local(): lax.all_to_all(share, BOTH, 0, 0, tiled=True).reshape(128 * 24, 128)]
    unnamed x16 -> x20, local copies, waits for them, and re-layouts: 2.53 us -> 10.8 us
    all_to_all x2 -> x1, waiting for transfers between devices: 0.01 us -> 6.27 us  [local(): lax.all_to_all(share, BOTH, 0, 0, tiled=True).reshape(128 * 24, 128)]
    all_to_all x1, starting transfers between devices: 10.2 us -> 4.7 us  [local(): lax.all_to_all(errors.reshape(128, 48, 128), BOTH, 0, 0, tiled=True)]
    broadcast_in_dim x2 -> x0, local copies, waits for them, and re-layouts: 3.46 us -> none  [the longest x1 1.73 us: local(): jnp.broadcast_to(shown.reshape(1, 16, 128), (128, 16, 128))]
    all_to_all x1, waiting for transfers between devices: 37.4 us -> 40.8 us  [local(): lax.all_to_all(errors.reshape(128, 48, 128), BOTH, 0, 0, tiled=True)]
  transfers between devices with their start and end apart: 4 -> 3, of which waited for: 2 -> 3; matrix products, arithmetic and copies ran while one was open for 0% -> 1% of each run, Pallas kernels for 36% -> 9%
where the time goes in v2:
time: 171 us
  waiting for transfers between devices  81.9 us (48%)
  Pallas kernels  52.1 us (30%)
  starting transfers between devices  19.9 us (12%)
  local copies, waits for them, and re-layouts  12.5 us (7%)
  other arithmetic  3.33 us (2%)
    all_to_all x1, waiting for transfers between devices, local(): lax.all_to_all(errors.reshape(128, 48, 128), BOTH, 0, 0, tiled=True)  40.8 us
    all_to_all x1, waiting for transfers between devices, local(): lax.all_to_all(sent.reshape(128, CH, 128), BOTH, 0, 0, tiled=True)  34.9 us
    pallas_call x1, Pallas kernels, local(): call(resid_body, (jax.ShapeDtypeStruct((512, 8, 128), F32), jax.ShapeDtyp...  16.7 us
    pallas_call x1, Pallas kernels, local(): call(error_body, jax.ShapeDtypeStruct((128 * 48, 128), F32), [pltpu.VMEM(...  14.2 us
    pallas_call x1, Pallas kernels, local(): call(sums_body, jax.ShapeDtypeStruct((32, 8, 128), F32), [pltpu.VMEM((256...  12.6 us
    all_to_all x1, starting transfers between devices, local(): lax.all_to_all(sent.reshape(128, CH, 128), BOTH, 0, 0, tiled=True)  11.5 us
    unnamed x20, local copies, waits for them, and re-layouts  10.8 us
    all_to_all x1, waiting for transfers between devices, local(): lax.all_to_all(share, BOTH, 0, 0, tiled=True).reshape(128 * 24, 128)  6.27 us
  transfers between devices with their start and end apart: 3, of which 3 were waited for; matrix products, arithmetic and copies ran while one was open for 1% of the time, Pallas kernels for 9%

profile of v2, /device:TPU:1, one launch (start us, length us, event | category | flops | bytes accessed | tf_op | source)
XLA Modules:
  0.0 170.5 jit_solution(981290999192454080)
XLA Ops:
  0.6 0.0 copy-start
  0.7 0.9 convert_reduce_fusion
  1.6 0.7 multiply_add_fusion
  2.2 0.1 pad.9.clone
  2.3 0.8 reshape.39
  3.1 0.1 pad_add_fusion.place
  3.2 0.7 add_bitcast_fusion
  3.9 0.1 add_convert_fusion.meta
  4.0 1.4 copy-done.5
  5.4 1.0 copy-done.6
  6.4 0.9 copy-done.7
  7.3 3.3 %shard_map.94 = f32[5120,128]{1,0:T(8,128)} custom-call(s32[2]{0:T(128)S(1)} %pad_add_fusion.place, f32[512,768]{1,0:T(8,128)S(1)} %bitcast.23, s32[512,96]{1,0:T(8,128)S(1)} %bitcast.24, f32[8,128]{1,0:T(8,128)S(1)} %add_convert_fusion.meta, f32[128,768]{1,0:T(8,128)S(1)} %copy-done.6), custom_call_target="tpu_custom_call" | custom-call | bytes 5242880 | tf_op jit(solution)/shard_map/pallas_call | solution.py:365
  10.6 11.5 %all-to-all-start = ((f32[128,40,128]{2,1,0:T(8,128)}), f32[128,40,128]{2,1,0:T(8,128)S(1)}, u32[]{:S(2)}, u32[]{:S(2)}) async-start(f32[128,40,128]{2,1,0:T(8,128)} %bitcast.7), calls=%async_computation | async-start | bytes 5242880 | tf_op jit(solution)/shard_map/all_to_all | solution.py:375
  22.1 0.1 constant_dynamic-slice_fusion
  22.2 0.7 copy.13
  22.9 0.9 select_maximum_fusion.book
  23.8 34.9 %all-to-all-done = f32[128,40,128]{2,1,0:T(8,128)S(1)} async-done(((f32[128,40,128]{2,1,0:T(8,128)}), f32[128,40,128]{2,1,0:T(8,128)S(1)}, u32[]{:S(2)}, u32[]{:S(2)}) %all-to-all-start) | async-done | bytes 2621472 | tf_op jit(solution)/shard_map/all_to_all | solution.py:375
  58.7 12.6 %shard_map.95.fresh = f32[32,8,128]{2,1,0:T(8,128)S(1)} custom-call(f32[5120,128]{1,0:T(8,128)S(1)} %bitcast.20), custom_call_target="tpu_custom_call" | custom-call | flops 8589934592 | bytes 3145728 | tf_op jit(solution)/shard_map/pallas_call | solution.py:377
  71.3 16.7 %shard_map.96 = (f32[512,8,128]{2,1,0:T(8,128)S(1)}, f32[4,8,128]{2,1,0:T(8,128)S(1)}, f32[128,24,128]{2,1,0:T(8,128)S(1)}) custom-call(s32[2]{0:T(128)S(1)} %pad_add_fusion.place, f32[5120,128]{1,0:T(8,128)S(1)} %bitcast.21, f32[32,8,128]{2,1,0:T(8,128)S(1)} %shard_map.95.fresh, f32[4,8,128]{2,1,0:T(8,128)S(1)} %select_maximum_fusion.book), custom_call_target="tpu_custom_call" | custom-call | flops 8589934592 | bytes 6291456 | tf_op jit(solution)/shard_map/pallas_call | solution.py:388
  88.0 0.0 copy-start.4
  88.0 1.1 copy-done.4
  89.1 1.3 copy-done.8
  90.5 3.7 %all-to-all-start.1 = ((f32[128,24,128]{2,1,0:T(8,128)}), f32[128,24,128]{2,1,0:T(8,128)S(1)}, u32[]{:S(2)}, u32[]{:S(2)}) async-start(f32[128,24,128]{2,1,0:T(8,128)} %copy-done.4), calls=%async_computation.1 | async-start | bytes 3145728 | tf_op jit(solution)/shard_map/all_to_all | solution.py:402
  94.2 1.7 %copy-done.3 = f32[128,40,128]{2,1,0:T(8,128)S(1)} copy-done((f32[128,40,128]{2,1,0:T(8,128)S(1)}, f32[128,40,128]{2,1,0:T(8,128)}, u32[]{:S(2)}) %copy-start.3) | copy-done | bytes 2621464
  95.9 1.6 copy-done.9
  97.5 14.2 %shard_map.98 = f32[6144,128]{1,0:T(8,128)S(1)} custom-call(s32[2]{0:T(128)S(1)} %pad_add_fusion.place, f32[5120,128]{1,0:T(8,128)S(1)} %bitcast.22, f32[512,8,128]{2,1,0:T(8,128)S(1)} %copy-done.9, f32[4,8,128]{2,1,0:T(8,128)S(1)} %get-tuple-element.11.table), custom_call_target="tpu_custom_call" | custom-call | flops 8589934592 | bytes 8388608 | tf_op jit(solution)/shard_map/pallas_call | solution.py:404
  111.7 1.7 copy-done.1
  113.4 6.3 %all-to-all-done.1 = f32[128,24,128]{2,1,0:T(8,128)S(1)} async-done(((f32[128,24,128]{2,1,0:T(8,128)}), f32[128,24,128]{2,1,0:T(8,128)S(1)}, u32[]{:S(2)}, u32[]{:S(2)}) %all-to-all-start.1) | async-done | bytes 1572896 | tf_op jit(solution)/shard_map/all_to_all | solution.py:402
  119.7 4.7 %all-to-all-start.2 = ((f32[128,48,128]{2,1,0:T(8,128)}), f32[128,48,128]{2,1,0:T(8,128)}, u32[]{:S(2)}, u32[]{:S(2)}) async-start(f32[128,48,128]{2,1,0:T(8,128)} %bitcast.19), calls=%async_computation.2 | async-start | bytes 6291456 | tf_op jit(solution)/shard_map/all_to_all | solution.py:414
  124.4 1.3 shard_map.97
  125.7 40.8 %all-to-all-done.2 = f32[128,48,128]{2,1,0:T(8,128)} async-done(((f32[128,48,128]{2,1,0:T(8,128)}), f32[128,48,128]{2,1,0:T(8,128)}, u32[]{:S(2)}, u32[]{:S(2)}) %all-to-all-start.2) | async-done | bytes 3145760 | tf_op jit(solution)/shard_map/all_to_all | solution.py:414
  166.4 4.1 %shard_map.99 = bf16[128,8,768]{2,1,0:T(8,128)(2,1)} custom-call(f32[6144,128]{1,0:T(8,128)} %bitcast.14.recv), custom_call_target="tpu_custom_call" | custom-call | bytes 5242880 | tf_op jit(solution)/shard_map/pallas_call | solution.py:423
  (11 shorter events, 0.0 us)
Async XLA Ops:
  0.6 21.5 %copy-start = (f32[256,768]{1,0:T(8,128)S(1)}, f32[256,768]{1,0:T(8,128)}, u32[]{:S(2)}) copy-start(f32[256,768]{1,0:T(8,128)} %param.13) | copy-start | bytes 2359300
  4.0 1.4 copy-start.5
  5.4 1.0 copy-start.6
  6.4 0.9 copy-start.7
  10.6 48.1 %all-to-all-start = ((f32[128,40,128]{2,1,0:T(8,128)}), f32[128,40,128]{2,1,0:T(8,128)S(1)}, u32[]{:S(2)}, u32[]{:S(2)}) async-start(f32[128,40,128]{2,1,0:T(8,128)} %bitcast.7), calls=%async_computation | async-start | bytes 5242880 | tf_op jit(solution)/shard_map/all_to_all | solution.py:375
  58.7 12.6 %copy-start.2 = (f32[128,40,128]{2,1,0:T(8,128)}, f32[128,40,128]{2,1,0:T(8,128)S(1)}, u32[]{:S(2)}) copy-start(f32[128,40,128]{2,1,0:T(8,128)S(1)} %all-to-all-done) | copy-start | bytes 7864324
  88.0 1.1 copy-start.4
  89.1 1.3 copy-start.8
  90.5 29.2 %all-to-all-start.1 = ((f32[128,24,128]{2,1,0:T(8,128)}), f32[128,24,128]{2,1,0:T(8,128)S(1)}, u32[]{:S(2)}, u32[]{:S(2)}) async-start(f32[128,24,128]{2,1,0:T(8,128)} %copy-done.4), calls=%async_computation.1 | async-start | bytes 3145728 | tf_op jit(solution)/shard_map/all_to_all | solution.py:402
  94.1 1.7 %copy-start.3 = (f32[128,40,128]{2,1,0:T(8,128)S(1)}, f32[128,40,128]{2,1,0:T(8,128)}, u32[]{:S(2)}) copy-start(f32[128,40,128]{2,1,0:T(8,128)} %copy-done.2) | copy-start | bytes 7864324
  95.9 1.6 copy-start.9
  111.7 1.7 copy-start.1
  119.7 46.8 %all-to-all-start.2 = ((f32[128,48,128]{2,1,0:T(8,128)}), f32[128,48,128]{2,1,0:T(8,128)}, u32[]{:S(2)}, u32[]{:S(2)}) async-start(f32[128,48,128]{2,1,0:T(8,128)} %bitcast.19), calls=%async_computation.2 | async-start | bytes 6291456 | tf_op jit(solution)/shard_map/all_to_all | solution.py:414

commit v3 on v2

--- a/solution.py
+++ b/solution.py
@@ -11,15 +11,16 @@
 BF16 = jnp.bfloat16
 
 CH = 40
+EC = 72
 FIRST = (0, 0, 1, 2)
 SECOND = (0, 1, 2, 2)
 
 
-def call(body, out, scratch, mib, scalar=False, operands=1, flops=0, moved=0):
-    vmem = pl.BlockSpec(memory_space=pltpu.VMEM)
+def call(body, ins, outs, out, scratch, mib, flops=0, moved=0):
     return pl.pallas_call(
         body,
-        in_specs=([pl.BlockSpec(memory_space=pltpu.SMEM)] if scalar else []) + [vmem] * operands,
+        in_specs=ins,
+        out_specs=outs,
         out_shape=out,
         scratch_shapes=list(scratch),
         compiler_params=pltpu.CompilerParams(vmem_limit_bytes=mib << 20),
@@ -48,28 +49,35 @@
     return hi, x - hi
 
 
-def send_body(place, corpus, codes, meta, cent, out, turned, words, rows_s, codes_s, rows_c):
-    codes_s[:, 0:96] = codes[...].astype(F32)
-    for w in range(6):
-        rows_c[w] = corpus[:, w * 128 : (w + 1) * 128]
-    for p in range(4):
-        for w in range(6):
-            for h in range(2):
-                rows_s[h * 64 : (h + 1) * 64, :] = rows_c[w, pl.ds(2 * p + h, 64, stride=8), :]
-            turned[w * 128 : (w + 1) * 128, :] = rows_s[...].T
-        for c in range(6):
-            out[pl.ds(p * 8 + c, 128, stride=CH), :] = turned[pl.ds(c, 128, stride=6), :]
-        for h in range(2):
-            rows_s[h * 64 : (h + 1) * 64, :] = codes_s[pl.ds(2 * p + h, 64, stride=8), :]
-        words[...] = rows_s[...].T
-        for j in range(4):
-            for k, pick in ((6, FIRST[j]), (7, SECOND[j])):
-                out[pl.ds(j * CH + p * 8 + k, 32, stride=4 * CH), :] = words[pl.ds(pick, 32, stride=3), :]
+def send_body(place, corpus, codes, cent, dest, counts, assign, out, turned, words, rows_s, codes_s, rows_c, codes_i, cent_s, sems):
+    moves = [pltpu.make_async_copy(corpus.at[:, pl.ds(w * 128, 128)], rows_c.at[w], sems.at[w]) for w in range(6)]
+    moves.append(pltpu.make_async_copy(codes, codes_i, sems.at[6]))
+    moves.append(pltpu.make_async_copy(cent, cent_s, sems.at[7]))
+    for move in moves:
+        move.start()
+    lane = lanes((1, 128))
+    here = dest[...].astype(F32)
+    here = jnp.broadcast_to(jnp.concatenate([here, here], 1), (128, 128))
+    there = here.T
+    before = (there == here) & (subs((128, 128)) < lanes((128, 128)))
+    rank = jnp.sum(jnp.where(before, 1.0, 0.0), axis=0, keepdims=True)
+    slot = here[0:1, :] * 4.0 + rank
+    used = counts[...].astype(F32)
+    used = jnp.concatenate([used, used], 1)
+    labels = assign[...].astype(F32)
+    labels = jnp.concatenate([labels, labels], 1)
+    infos = [jnp.where(lane < 64, labels[2 * p : 2 * p + 1, :], labels[2 * p + 1 : 2 * p + 2, :]) for p in range(4)]
+    infos.append(jnp.where(lane < 64, slot, used))
     for k in range(5):
-        out[pl.ds(32 + k, 128, stride=CH), :] = jnp.broadcast_to(meta[k : k + 1, :], (128, 128))
+        out[pl.ds(32 + k, 128, stride=CH), :] = jnp.broadcast_to(infos[k], (128, 128))
+    out[pl.ds(39, 128, stride=CH), :] = jnp.zeros((128, 128), F32)
+    moves[6].wait()
+    codes_s[:, 0:96] = codes_i[...].astype(F32)
+    codes_s[:, 96:128] = jnp.zeros((512, 32), F32)
+    moves[7].wait()
     start = pl.multiple_of(place[1] * 32, 32)
     for w in range(6):
-        rows_s[0:32, :] = cent[pl.ds(start, 32), w * 128 : (w + 1) * 128]
+        rows_s[0:32, :] = cent_s[pl.ds(start, 32), w * 128 : (w + 1) * 128]
         rows_s[32:128, :] = jnp.zeros((96, 128), F32)
         turned[w * 128 : (w + 1) * 128, :] = rows_s[...].T
     parts = [turned[pl.ds(c, 128, stride=6), :] for c in range(6)]
@@ -78,7 +86,21 @@
         for i, c in enumerate(cols[1:], 1):
             row = row + pltpu.roll(parts[c], 32 * i, 1)
         out[pl.ds(32 + k, 128, stride=CH), :] = row
-    out[pl.ds(39, 128, stride=CH), :] = jnp.zeros((128, 128), F32)
+    for p in range(4):
+        for h in range(2):
+            rows_s[h * 64 : (h + 1) * 64, :] = codes_s[pl.ds(2 * p + h, 64, stride=8), :]
+        words[...] = rows_s[...].T
+        for j in range(4):
+            for k, pick in ((6, FIRST[j]), (7, SECOND[j])):
+                out[pl.ds(j * CH + p * 8 + k, 32, stride=4 * CH), :] = words[pl.ds(pick, 32, stride=3), :]
+        for w in range(6):
+            if p == 0:
+                moves[w].wait()
+            for h in range(2):
+                rows_s[h * 64 : (h + 1) * 64, :] = rows_c[w, pl.ds(2 * p + h, 64, stride=8), :]
+            turned[w * 128 : (w + 1) * 128, :] = rows_s[...].T
+        for c in range(6):
+            out[pl.ds(p * 8 + c, 128, stride=CH), :] = turned[pl.ds(c, 128, stride=6), :]
 
 
 def row_info(tile):
@@ -95,7 +117,7 @@
 LOOK_SRC = 8
 
 
-def sums_body(recv, out, acc):
+def sums_part(recv, out, acc):
     acc[...] = jnp.zeros((256, 256), F32)
     sub8 = subs((8, 128))
     digits = subs((256, 128)).astype(F32).astype(BF16)
@@ -154,7 +176,7 @@
     return a, b
 
 
-def resid_body(place, recv, fresh, book, resid, table, share, left, acc):
+def resid_part(place, recv, fresh, book, resid, table, left, acc):
     first = place[0]
     sub8 = subs((8, 128))
     lane = lanes((8, 128))
@@ -222,17 +244,10 @@
         made.append(new + pltpu.roll(new, 64, 1))
     shown = [jnp.where(lane < 64, made[0], made[1]), jnp.where(lane < 64, made[2], made[3])]
 
-    def spread(s, carry):
-        for g in range(4):
-            share[s * 4 + g, 0:8, :] = fresh[s]
-            share[s * 4 + g, 8:16, :] = shown[0]
-            share[s * 4 + g, 16:24, :] = shown[1]
-        return carry
-
-    lax.fori_loop(0, 32, spread, 0)
-
-
-def error_body(place, recv, resid, table, out, left, spread, mixed):
+    return shown
+
+
+def error_part(place, recv, fresh, shown, resid, table, out, left, spread, mixed, stage, sems):
     first = place[0]
     sub8 = subs((8, 128))
     lane = lanes((8, 128))
@@ -313,115 +328,148 @@
 
     lax.fori_loop(0, 8, mix, 0)
 
+    def move(t):
+        rows = pl.ds(pl.multiple_of(t * 4 * EC, 8), 4 * EC)
+        return pltpu.make_async_copy(stage.at[rows], out.at[rows], sems.at[t])
+
     def finish(t, carry):
         for h in range(2):
             tile = mixed[t, :, h * 128 : (h + 1) * 128].T
             for g2 in range(2):
+                base = pl.multiple_of((t * 4 + 2 * h + g2) * EC, 8)
                 for r in range(8):
-                    out[pl.ds((t * 4 + 2 * h + g2) * 48 + r, 6, stride=8), :] = tile[g2 * 64 + r * 8 : g2 * 64 + r * 8 + 6, :]
+                    stage[pl.ds(base + r, 6, stride=8), :] = tile[g2 * 64 + r * 8 : g2 * 64 + r * 8 + 6, :]
+                stage[pl.ds(base + 48, 8), :] = fresh[t]
+                stage[pl.ds(base + 56, 8), :] = shown[0]
+                stage[pl.ds(base + 64, 8), :] = shown[1]
+        move(t).start()
         return carry
 
     lax.fori_loop(0, 32, finish, 0)
 
-
-def place_body(recv, out, turned):
-    for r in range(8):
-        for w in range(6):
-            turned[w, pl.ds(r, 128, stride=8), :] = recv[pl.ds(w * 1024 + r, 128, stride=8), :].T
-    for w in range(6):
-        out[:, :, w * 128 : (w + 1) * 128] = turned[w].reshape(128, 8, 128).astype(BF16)
-
-
-def columns_body(recv, centroids, book, turned):
+    def settle(t, carry):
+        move(t).wait()
+        return carry
+
+    lax.fori_loop(0, 32, settle, 0)
+
+
+def main_body(place, recv, book, out, sums, fresh, left, csum, resid, table, words, spread, mixed, stage, sems):
+    sums_part(recv, fresh, sums)
+    shown = resid_part(place, recv, fresh, book, resid, table, left, csum)
+    error_part(place, recv, fresh, shown, resid, table, out, words, spread, mixed, stage, sems)
+
+
+def place_body(landed, out, centroids, book, buf, extra, turned, cols, sems):
+    moves = [
+        pltpu.make_async_copy(landed.at[pl.ds(16 * k, 16), pl.ds(0, 48)], buf.at[pl.ds(16 * k, 16)], sems.at[k])
+        for k in range(8)
+    ]
+    moves.append(pltpu.make_async_copy(landed.at[:, pl.ds(48, 24)], extra, sems.at[8]))
+    for move in moves[8:] + moves[:8]:
+        move.start()
+    moves[8].wait()
+    flat = extra.reshape(128 * 24, 128)
     for h in range(3):
         for c in range(6):
-            turned[pl.ds(c, 128, stride=6), :] = recv[pl.ds(h * 8 + c, 128, stride=24), :]
+            cols[pl.ds(c, 128, stride=6), :] = flat[pl.ds(h * 8 + c, 128, stride=24), :]
         for w in range(6):
-            tile = turned[w * 128 : (w + 1) * 128, :].T
+            tile = cols[w * 128 : (w + 1) * 128, :].T
             if h == 0:
                 centroids[:, w * 128 : (w + 1) * 128] = tile
             else:
                 book[(h - 1) * 128 : h * 128, w * 128 : (w + 1) * 128] = tile
-
-
-def slot_ranks(dest):
-    count = dest.shape[0]
-    order = jnp.arange(count, dtype=jnp.int32)
-    same = (dest[:, None] == dest[None, :]) & (order[None, :] < order[:, None])
-    return jnp.sum(same.astype(jnp.int32), axis=1)
+    flat = buf.reshape(128 * 48, 128)
+    ready = 0
+    for w in range(6):
+        need = (128 * w + 127) // 6 // 16 + 1
+        for k in range(ready, need):
+            moves[k].wait()
+        ready = need
+        for r in range(8):
+            turned[w, pl.ds(r, 128, stride=8), :] = flat[pl.ds(w * 1024 + r, 128, stride=8), :].T
+        out[:, :, w * 128 : (w + 1) * 128] = turned[w].reshape(128, 8, 128).astype(BF16)
 
 
 def local(corpus, block_rows, targets, assign, codes, centroids, codebook):
     grp = lax.axis_index("grp")
     me = lax.axis_index("shard") * 4 + grp
     first = jnp.where(grp == 1, 2, jnp.where(grp == 2, 4, 6)).astype(jnp.int32)
-    dest = targets[:, 0]
-    slot = dest * 4 + slot_ranks(dest)
-    meta = jnp.concatenate(
-        [assign.T.reshape(4, 128), jnp.concatenate([slot, block_rows]).reshape(1, 128), jnp.zeros((3, 128), jnp.int32)], 0
-    ).astype(F32)
     place = jnp.stack([first, grp])
+    vmem, hbm, smem = (pl.BlockSpec(memory_space=m) for m in (pltpu.VMEM, pltpu.HBM, pltpu.SMEM))
 
     sent = call(
         send_body,
+        [smem, hbm, hbm, hbm, vmem, vmem, vmem],
+        vmem,
         jax.ShapeDtypeStruct((128 * CH, 128), F32),
-        [pltpu.VMEM((768, 128), F32), pltpu.VMEM((128, 128), F32), pltpu.VMEM((128, 128), F32), pltpu.VMEM((512, 128), F32),
-         pltpu.VMEM((6, 512, 128), F32)],
+        [
+            pltpu.VMEM((768, 128), F32),
+            pltpu.VMEM((128, 128), F32),
+            pltpu.VMEM((128, 128), F32),
+            pltpu.VMEM((512, 128), F32),
+            pltpu.VMEM((6, 512, 128), F32),
+            pltpu.VMEM((512, 96), jnp.int32),
+            pltpu.VMEM((128, 768), F32),
+            pltpu.SemaphoreType.DMA((8,)),
+        ],
         16,
-        scalar=True,
-        operands=4,
         moved=5 << 20,
-    )(place, corpus.reshape(512, 768), codes.reshape(512, 96), meta, centroids)
+    )(
+        place,
+        corpus.reshape(512, 768),
+        codes.reshape(512, 96),
+        centroids,
+        targets.reshape(1, 64),
+        block_rows.reshape(1, 64),
+        assign.T,
+    )
     recv = lax.all_to_all(sent.reshape(128, CH, 128), BOTH, 0, 0, tiled=True).reshape(128 * CH, 128)
-
-    fresh = call(
-        sums_body,
-        jax.ShapeDtypeStruct((32, 8, 128), F32),
-        [pltpu.VMEM((256, 256), F32)],
-        12,
-        flops=1 << 33,
-        moved=3 << 20,
-    )(recv)
 
     old = lax.dynamic_slice(codebook, (0, 6 * me), (256, 6)).T.reshape(6, 4, 64).transpose(1, 0, 2)
     old = jnp.pad(jnp.concatenate([old, old], 2), ((0, 0), (0, 2), (0, 0)))
-    resid, table, share = call(
-        resid_body,
+    errors = call(
+        main_body,
+        [smem, vmem, vmem],
+        hbm,
+        jax.ShapeDtypeStruct((128 * EC, 128), F32),
+        [
+            pltpu.VMEM((256, 256), F32),
+            pltpu.VMEM((32, 8, 128), F32),
+            pltpu.VMEM((256, 256), BF16),
+            pltpu.VMEM((64, 128), F32),
+            pltpu.VMEM((512, 8, 128), F32),
+            pltpu.VMEM((4, 8, 128), F32),
+            pltpu.VMEM((64, 128), BF16),
+            pltpu.VMEM((16, 256, 512), BF16),
+            pltpu.VMEM((32, 128, 256), F32),
+            pltpu.VMEM((128 * EC, 128), F32),
+            pltpu.SemaphoreType.DMA((32,)),
+        ],
+        32,
+        flops=1 << 34,
+        moved=8 << 20,
+    )(place, recv, old)
+    landed = lax.all_to_all(errors.reshape(128, EC, 128), BOTH, 0, 0, tiled=True)
+
+    moved_error, new_centroids, new_codebook = call(
+        place_body,
+        [hbm],
+        (vmem, vmem, vmem),
         (
-            jax.ShapeDtypeStruct((512, 8, 128), F32),
-            jax.ShapeDtypeStruct((4, 8, 128), F32),
-            jax.ShapeDtypeStruct((128, 24, 128), F32),
+            jax.ShapeDtypeStruct((128, 8, 768), BF16),
+            jax.ShapeDtypeStruct((128, 768), F32),
+            jax.ShapeDtypeStruct((256, 768), F32),
         ),
-        [pltpu.VMEM((256, 256), BF16), pltpu.VMEM((64, 128), F32)],
-        16,
-        scalar=True,
-        operands=3,
-        flops=1 << 33,
-        moved=6 << 20,
-    )(place, recv, fresh, old)
-    shared = lax.all_to_all(share, BOTH, 0, 0, tiled=True).reshape(128 * 24, 128)
-
-    errors = call(
-        error_body,
-        jax.ShapeDtypeStruct((128 * 48, 128), F32),
-        [pltpu.VMEM((64, 128), BF16), pltpu.VMEM((16, 256, 512), BF16), pltpu.VMEM((32, 128, 256), F32)],
+        [
+            pltpu.VMEM((128, 48, 128), F32),
+            pltpu.VMEM((128, 24, 128), F32),
+            pltpu.VMEM((6, 1024, 128), F32),
+            pltpu.VMEM((768, 128), F32),
+            pltpu.SemaphoreType.DMA((9,)),
+        ],
         24,
-        scalar=True,
-        operands=3,
-        flops=1 << 33,
-        moved=8 << 20,
-    )(place, recv, resid, table)
-    landed = lax.all_to_all(errors.reshape(128, 48, 128), BOTH, 0, 0, tiled=True).reshape(128 * 48, 128)
-
-    new_centroids, new_codebook = call(
-        columns_body,
-        (jax.ShapeDtypeStruct((128, 768), F32), jax.ShapeDtypeStruct((256, 768), F32)),
-        [pltpu.VMEM((768, 128), F32)],
-        12,
-        moved=3 << 20,
-    )(shared)
-    moved_error = call(
-        place_body, jax.ShapeDtypeStruct((128, 8, 768), BF16), [pltpu.VMEM((6, 1024, 128), F32)], 16, moved=5 << 20
+        moved=7 << 20,
     )(landed)
     return (new_centroids, moved_error, new_codebook)
 

time: 171 us -> 174 us (1.018)
  blocking collectives: 0 us -> 62.3 us
  waiting for transfers between devices: 81.9 us -> 34.9 us
  starting transfers between devices: 19.9 us -> 11.5 us
  local copies, waits for them, and re-layouts: 12.5 us -> 6.22 us
  Pallas kernels: 52.1 us -> 57.2 us
  other arithmetic: 3.33 us -> 0.94 us
    all_to_all x0 -> x1, blocking collectives: none -> 62.3 us  [local(): lax.all_to_all(errors.reshape(128, EC, 128), BOTH, 0, 0, tiled=True)]
    all_to_all x2 -> x0, waiting for transfers between devices: 47 us -> none  [the longest x1 40.8 us: local(): lax.all_to_all(errors.reshape(128, 48, 128), BOTH, 0, 0, tiled=True)]
    all_to_all x2 -> x0, starting transfers between devices: 8.37 us -> none  [the longest x1 4.7 us: local(): lax.all_to_all(errors.reshape(128, 48, 128), BOTH, 0, 0, tiled=True)]
    unnamed x20 -> x14, local copies, waits for them, and re-layouts: 10.8 us -> 5.41 us
    pallas_call x6 -> x3, Pallas kernels: 52.1 us -> 57.2 us  [the longest x1 49.2 us: local(): call(main_body, [smem, vmem, vmem], hbm, jax.ShapeDtypeStruct((128 * EC,...]
  transfers between devices with their start and end apart: 3 -> 1, of which waited for: 3 -> 1; matrix products, arithmetic and copies ran while one was open for 1% -> 1% of each run, Pallas kernels for 9% -> 0%
where the time goes in v3:
time: 174 us
  blocking collectives  62.3 us (36%)
  Pallas kernels  57.2 us (33%)
  waiting for transfers between devices  34.9 us (20%)
  starting transfers between devices  11.5 us (7%)
  local copies, waits for them, and re-layouts  6.22 us (4%)
    all_to_all x1, blocking collectives, local(): lax.all_to_all(errors.reshape(128, EC, 128), BOTH, 0, 0, tiled=True)  62.3 us
    pallas_call x1, Pallas kernels, local(): call(main_body, [smem, vmem, vmem], hbm, jax.ShapeDtypeStruct((128 * EC,...  49.2 us
    all_to_all x1, waiting for transfers between devices, local(): lax.all_to_all(sent.reshape(128, CH, 128), BOTH, 0, 0, tiled=True)  34.9 us
    all_to_all x1, starting transfers between devices, local(): lax.all_to_all(sent.reshape(128, CH, 128), BOTH, 0, 0, tiled=True)  11.5 us
    unnamed x14, local copies, waits for them, and re-layouts  5.41 us
    pallas_call x1, Pallas kernels, local(): call(send_body, [smem, hbm, hbm, hbm, vmem, vmem, vmem], vmem, jax.ShapeD...  4.38 us
    pallas_call x1, Pallas kernels, local(): call(place_body, [hbm], (vmem, vmem, vmem), (jax.ShapeDtypeStruct((128, 8...  3.58 us
  transfers between devices with their start and end apart: 1, of which 1 were waited for; matrix products, arithmetic and copies ran while one was open for 1% of the time, Pallas kernels for 0%

profile of v3, /device:TPU:1, one launch (start us, length us, event | category | flops | bytes accessed | tf_op | source)
XLA Modules:
  0.0 173.7 jit_solution(4655854706326535443)
XLA Ops:
  0.6 0.0 copy-start
  0.7 0.1 pad_add_fusion.place
  0.7 0.0 copy-start.1
  0.7 1.5 copy-done.1
  2.2 0.0 copy-start.2
  2.2 1.0 copy-done.2
  3.2 0.0 copy-start.3
  3.2 0.9 copy-done.3
  4.1 0.0 copy-start.4
  4.1 0.7 copy-done.4
  4.8 0.0 copy-start.5
  4.8 0.7 copy-done.5
  5.5 0.0 copy-start.6
  5.5 0.7 copy-done.6
  6.1 4.4 %shard_map.94 = f32[5120,128]{1,0:T(8,128)} custom-call(s32[2]{0:T(128)S(1)} %pad_add_fusion.place, f32[512,768]{1,0:T(8,128)S(1)} %bitcast.16, s32[512,96]{1,0:T(8,128)S(1)} %bitcast.17, f32[128,768]{1,0:T(8,128)S(1)} %copy-done.2, s32[1,64]{1,0:T(1,128)S(1)} %bitcast.19, s32[1,64]{1,0:T(1,128)S(1)} %bitcast.20, s32[8,64]{1,0:T(8,128)S(1)} %bitcast.18), custom_call_target="tpu_custom_call" | custom-call | bytes 5242880 | tf_op jit(solution)/shard_map/pallas_call | solution.py:401
  10.5 11.5 %all-to-all-start = ((f32[128,40,128]{2,1,0:T(8,128)}), f32[128,40,128]{2,1,0:T(8,128)S(1)}, u32[]{:S(2)}, u32[]{:S(2)}) async-start(f32[128,40,128]{2,1,0:T(8,128)} %bitcast.7), calls=%async_computation | async-start | bytes 5242880 | tf_op jit(solution)/shard_map/all_to_all | solution.py:427
  22.0 0.0 copy-done
  22.1 0.1 constant_dynamic-slice_fusion
  22.2 0.7 copy.11
  22.9 0.9 select_maximum_fusion.book
  23.7 34.9 %all-to-all-done = f32[128,40,128]{2,1,0:T(8,128)S(1)} async-done(((f32[128,40,128]{2,1,0:T(8,128)}), f32[128,40,128]{2,1,0:T(8,128)S(1)}, u32[]{:S(2)}, u32[]{:S(2)}) %all-to-all-start) | async-done | bytes 2621472 | tf_op jit(solution)/shard_map/all_to_all | solution.py:427
  58.6 49.2 %shard_map.95 = f32[9216,128]{1,0:T(8,128)S(1)} custom-call(s32[2]{0:T(128)S(1)} %pad_add_fusion.place, f32[5120,128]{1,0:T(8,128)S(1)} %bitcast.15, f32[4,8,128]{2,1,0:T(8,128)S(1)} %select_maximum_fusion.book), custom_call_target="tpu_custom_call" | custom-call | flops 17179869184 | bytes 8388608 | tf_op jit(solution)/shard_map/pallas_call | solution.py:431
  107.9 62.3 %all_to_all.10.landed = f32[128,72,128]{2,1,0:T(8,128)S(1)} all-to-all(f32[128,72,128]{2,1,0:T(8,128)S(1)} %bitcast.14), channel_id=1, replica_groups=mesh['shard'=32,'grp'=4] {'shard','grp'}, dimensions={0} | all-to-all | bytes 9437184 | tf_op jit(solution)/shard_map/all_to_all | solution.py:453
  170.2 3.6 %shard_map.96 = (bf16[128,8,768]{2,1,0:T(8,128)(2,1)}, f32[128,768]{1,0:T(8,128)}, f32[256,768]{1,0:T(8,128)}) custom-call(f32[128,72,128]{2,1,0:T(8,128)S(1)} %all_to_all.10.landed), custom_call_target="tpu_custom_call" | custom-call | bytes 7340032 | tf_op jit(solution)/shard_map/pallas_call | solution.py:455
Async XLA Ops:
  0.6 21.4 %copy-start = (f32[256,768]{1,0:T(8,128)S(1)}, f32[256,768]{1,0:T(8,128)}, u32[]{:S(2)}) copy-start(f32[256,768]{1,0:T(8,128)} %param.13) | copy-start | bytes 2359300
  0.7 1.5 copy-start.1
  2.2 1.0 copy-start.2
  3.2 0.9 copy-start.3
  4.1 0.7 copy-start.4
  4.8 0.7 copy-start.5
  5.5 0.7 copy-start.6
  10.5 48.1 %all-to-all-start = ((f32[128,40,128]{2,1,0:T(8,128)}), f32[128,40,128]{2,1,0:T(8,128)S(1)}, u32[]{:S(2)}, u32[]{:S(2)}) async-start(f32[128,40,128]{2,1,0:T(8,128)} %bitcast.7), calls=%async_computation | async-start | bytes 5242880 | tf_op jit(solution)/shard_map/all_to_all | solution.py:427

commit v4 on v3

--- a/solution.py
+++ b/solution.py
@@ -113,7 +113,8 @@
 
 
 GRP_SRC = 32
-RES_SRC = 16
+RES_SRC = 32
+SEND_MIB = 56
 LOOK_SRC = 8
 
 
@@ -167,7 +168,7 @@
         out[s] = jnp.where(sub8 < 6, fresh, 0.0)
         return carry
 
-    lax.fori_loop(0, 32, finish, 0)
+    lax.fori_loop(0, 32, finish, 0, unroll=4)
 
 
 def code_digits(x, first, second_cols, used):
@@ -256,7 +257,10 @@
     for sel in range(4):
         hi, lo = split(table[sel])
         left[sel * 16 : (sel + 1) * 16, :] = jnp.concatenate([hi, lo], 0).astype(BF16)
-    spread[...] = jnp.zeros(spread.shape, BF16)
+    for g in range(4):
+        for other in range(4):
+            if other != g:
+                spread[:, g * 64 : (g + 1) * 64, other * 128 : (other + 1) * 128] = jnp.zeros((16, 64, 128), BF16)
 
     def look(i, carry):
         hot, useds = [], []
@@ -298,7 +302,7 @@
             spread[i, g * 64 : (g + 1) * 64, g * 128 : (g + 1) * 128] = jnp.concatenate(rows, 0).astype(BF16)
         return carry
 
-    lax.fori_loop(0, 16, look, 0)
+    lax.fori_loop(0, 16, look, 0, unroll=2)
 
     spots = subs((256, 128)).astype(F32).astype(BF16)
     spot_lane = lanes((1, 128))
@@ -326,7 +330,7 @@
         mixed[:, pl.ds(sh * 16, 16), :] = got.reshape(32, 16, 256)
         return carry
 
-    lax.fori_loop(0, 8, mix, 0)
+    lax.fori_loop(0, 8, mix, 0, unroll=2)
 
     def move(t):
         rows = pl.ds(pl.multiple_of(t * 4 * EC, 8), 4 * EC)
@@ -345,7 +349,7 @@
         move(t).start()
         return carry
 
-    lax.fori_loop(0, 32, finish, 0)
+    lax.fori_loop(0, 32, finish, 0, unroll=8)
 
     def settle(t, carry):
         move(t).wait()
@@ -413,7 +417,7 @@
             pltpu.VMEM((128, 768), F32),
             pltpu.SemaphoreType.DMA((8,)),
         ],
-        16,
+        SEND_MIB,
         moved=5 << 20,
     )(
         place,

time: 174 us -> 166 us (0.954)
  local copies, waits for them, and re-layouts: 6.22 us -> 0.82 us
  Pallas kernels: 57.2 us -> 53.9 us
    unnamed x14 -> x4, local copies, waits for them, and re-layouts: 5.41 us -> 0.02 us
    pallas_call x1, Pallas kernels: 49.2 us -> 44.7 us  [local(): call(main_body, [smem, vmem, vmem], hbm, jax.ShapeDtypeStruct((128 * EC,...]
where the time goes in v4:
time: 166 us
  blocking collectives  62.2 us (37%)
  Pallas kernels  53.9 us (32%)
  waiting for transfers between devices  34.9 us (21%)
  starting transfers between devices  11.5 us (7%)
    all_to_all x1, blocking collectives, local(): lax.all_to_all(errors.reshape(128, EC, 128), BOTH, 0, 0, tiled=True)  62.2 us
    pallas_call x1, Pallas kernels, local(): call(main_body, [smem, vmem, vmem], hbm, jax.ShapeDtypeStruct((128 * EC,...  44.7 us
    all_to_all x1, waiting for transfers between devices, local(): lax.all_to_all(sent.reshape(128, CH, 128), BOTH, 0, 0, tiled=True)  34.9 us
    all_to_all x1, starting transfers between devices, local(): lax.all_to_all(sent.reshape(128, CH, 128), BOTH, 0, 0, tiled=True)  11.5 us
    pallas_call x1, Pallas kernels, local(): call(send_body, [smem, hbm, hbm, hbm, vmem, vmem, vmem], vmem, jax.ShapeD...  5.64 us
    pallas_call x1, Pallas kernels, local(): call(place_body, [hbm], (vmem, vmem, vmem), (jax.ShapeDtypeStruct((128, 8...  3.58 us
  transfers between devices with their start and end apart: 1, of which 1 were waited for; matrix products, arithmetic and copies ran while one was open for 1% of the time, Pallas kernels for 0%

profile of v4, /device:TPU:1, one launch (start us, length us, event | category | flops | bytes accessed | tf_op | source)
XLA Modules:
  0.0 165.6 jit_solution(8689568354933303345)
XLA Ops:
  0.6 0.0 copy-start
  0.7 0.6 pad_add_fusion.place
  1.2 5.6 %shard_map.94 = f32[5120,128]{1,0:T(8,128)} custom-call(s32[2]{0:T(128)} %pad_add_fusion.place, f32[512,768]{1,0:T(8,128)} %bitcast.17, s32[512,96]{1,0:T(8,128)} %bitcast.19, f32[128,768]{1,0:T(8,128)} %cent.1, s32[1,64]{1,0:T(1,128)} %bitcast.22, s32[1,64]{1,0:T(1,128)} %bitcast.23, s32[8,64]{1,0:T(8,128)} %bitcast.21), custom_call_target="tpu_custom_call" | custom-call | bytes 5242880 | tf_op jit(solution)/shard_map/pallas_call | solution.py:405
  6.9 0.0 copy-start.1
  6.9 11.5 %all-to-all-start = ((f32[128,40,128]{2,1,0:T(8,128)}), f32[128,40,128]{2,1,0:T(8,128)S(1)}, u32[]{:S(2)}, u32[]{:S(2)}) async-start(f32[128,40,128]{2,1,0:T(8,128)} %bitcast.16), calls=%async_computation | async-start | bytes 5242880 | tf_op jit(solution)/shard_map/all_to_all | solution.py:431
  18.4 0.0 copy-done
  18.4 0.1 constant_dynamic-slice_fusion
  18.5 0.7 copy.11
  19.2 0.9 select_maximum_fusion.book
  20.1 34.9 %all-to-all-done = f32[128,40,128]{2,1,0:T(8,128)S(1)} async-done(((f32[128,40,128]{2,1,0:T(8,128)}), f32[128,40,128]{2,1,0:T(8,128)S(1)}, u32[]{:S(2)}, u32[]{:S(2)}) %all-to-all-start) | async-done | bytes 2621472 | tf_op jit(solution)/shard_map/all_to_all | solution.py:431
  55.0 0.0 copy-done.1
  55.0 44.7 %shard_map.95 = f32[9216,128]{1,0:T(8,128)S(1)} custom-call(s32[2]{0:T(128)S(1)} %copy-done.1, f32[5120,128]{1,0:T(8,128)S(1)} %bitcast.15, f32[4,8,128]{2,1,0:T(8,128)S(1)} %select_maximum_fusion.book), custom_call_target="tpu_custom_call" | custom-call | flops 17179869184 | bytes 8388608 | tf_op jit(solution)/shard_map/pallas_call | solution.py:435
  99.8 62.2 %all_to_all.10.landed = f32[128,72,128]{2,1,0:T(8,128)S(1)} all-to-all(f32[128,72,128]{2,1,0:T(8,128)S(1)} %bitcast.14), channel_id=1, replica_groups=mesh['shard'=32,'grp'=4] {'shard','grp'}, dimensions={0} | all-to-all | bytes 9437184 | tf_op jit(solution)/shard_map/all_to_all | solution.py:457
  162.0 3.6 %shard_map.96 = (bf16[128,8,768]{2,1,0:T(8,128)(2,1)}, f32[128,768]{1,0:T(8,128)}, f32[256,768]{1,0:T(8,128)}) custom-call(f32[128,72,128]{2,1,0:T(8,128)S(1)} %all_to_all.10.landed), custom_call_target="tpu_custom_call" | custom-call | bytes 7340032 | tf_op jit(solution)/shard_map/pallas_call | solution.py:459
Async XLA Ops:
  0.6 17.8 %copy-start = (f32[256,768]{1,0:T(8,128)S(1)}, f32[256,768]{1,0:T(8,128)}, u32[]{:S(2)}) copy-start(f32[256,768]{1,0:T(8,128)} %param.13) | copy-start | bytes 2359300
  6.9 48.1 %copy-start.1 = (s32[2]{0:T(128)S(1)}, s32[2]{0:T(128)}, u32[]{:S(2)}) copy-start(s32[2]{0:T(128)} %pad_add_fusion.place) | copy-start | bytes 28
  6.9 48.1 %all-to-all-start = ((f32[128,40,128]{2,1,0:T(8,128)}), f32[128,40,128]{2,1,0:T(8,128)S(1)}, u32[]{:S(2)}, u32[]{:S(2)}) async-start(f32[128,40,128]{2,1,0:T(8,128)} %bitcast.16), calls=%async_computation | async-start | bytes 5242880 | tf_op jit(solution)/shard_map/all_to_all | solution.py:431

commit v5 on v4

--- a/solution.py
+++ b/solution.py
@@ -49,7 +49,9 @@
     return hi, x - hi
 
 
-def send_body(place, corpus, codes, cent, dest, counts, assign, out, turned, words, rows_s, codes_s, rows_c, codes_i, cent_s, sems):
+def send_body(place, corpus, codes, cent, dest, counts, assign, sent, turned, words, rows_s, codes_s, rows_c, codes_i, cent_s, stage, sems):
+    out = stage.reshape(128 * CH, 128)
+    leave = [pltpu.make_async_copy(stage.at[:, pl.ds(8 * p, 8)], sent.at[:, pl.ds(8 * p, 8)], sems.at[8 + p]) for p in range(5)]
     moves = [pltpu.make_async_copy(corpus.at[:, pl.ds(w * 128, 128)], rows_c.at[w], sems.at[w]) for w in range(6)]
     moves.append(pltpu.make_async_copy(codes, codes_i, sems.at[6]))
     moves.append(pltpu.make_async_copy(cent, cent_s, sems.at[7]))
@@ -86,6 +88,7 @@
         for i, c in enumerate(cols[1:], 1):
             row = row + pltpu.roll(parts[c], 32 * i, 1)
         out[pl.ds(32 + k, 128, stride=CH), :] = row
+    leave[4].start()
     for p in range(4):
         for h in range(2):
             rows_s[h * 64 : (h + 1) * 64, :] = codes_s[pl.ds(2 * p + h, 64, stride=8), :]
@@ -101,6 +104,9 @@
             turned[w * 128 : (w + 1) * 128, :] = rows_s[...].T
         for c in range(6):
             out[pl.ds(p * 8 + c, 128, stride=CH), :] = turned[pl.ds(c, 128, stride=6), :]
+        leave[p].start()
+    for copy in leave:
+        copy.wait()
 
 
 def row_info(tile):
@@ -302,7 +308,7 @@
             spread[i, g * 64 : (g + 1) * 64, g * 128 : (g + 1) * 128] = jnp.concatenate(rows, 0).astype(BF16)
         return carry
 
-    lax.fori_loop(0, 16, look, 0, unroll=2)
+    lax.fori_loop(0, 16, look, 0, unroll=4)
 
     spots = subs((256, 128)).astype(F32).astype(BF16)
     spot_lane = lanes((1, 128))
@@ -330,7 +336,7 @@
         mixed[:, pl.ds(sh * 16, 16), :] = got.reshape(32, 16, 256)
         return carry
 
-    lax.fori_loop(0, 8, mix, 0, unroll=2)
+    lax.fori_loop(0, 8, mix, 0, unroll=4)
 
     def move(t):
         rows = pl.ds(pl.multiple_of(t * 4 * EC, 8), 4 * EC)
@@ -405,8 +411,8 @@
     sent = call(
         send_body,
         [smem, hbm, hbm, hbm, vmem, vmem, vmem],
-        vmem,
-        jax.ShapeDtypeStruct((128 * CH, 128), F32),
+        hbm,
+        jax.ShapeDtypeStruct((128, CH, 128), F32),
         [
             pltpu.VMEM((768, 128), F32),
             pltpu.VMEM((128, 128), F32),
@@ -415,7 +421,8 @@
             pltpu.VMEM((6, 512, 128), F32),
             pltpu.VMEM((512, 96), jnp.int32),
             pltpu.VMEM((128, 768), F32),
-            pltpu.SemaphoreType.DMA((8,)),
+            pltpu.VMEM((128, CH, 128), F32),
+            pltpu.SemaphoreType.DMA((13,)),
         ],
         SEND_MIB,
         moved=5 << 20,
@@ -428,7 +435,7 @@
         block_rows.reshape(1, 64),
         assign.T,
     )
-    recv = lax.all_to_all(sent.reshape(128, CH, 128), BOTH, 0, 0, tiled=True).reshape(128 * CH, 128)
+    recv = lax.all_to_all(sent, BOTH, 0, 0, tiled=True).reshape(128 * CH, 128)
 
     old = lax.dynamic_slice(codebook, (0, 6 * me), (256, 6)).T.reshape(6, 4, 64).transpose(1, 0, 2)
     old = jnp.pad(jnp.concatenate([old, old], 2), ((0, 0), (0, 2), (0, 0)))

time: 166 us -> 165 us (level)
  no operation moved by 1% of the time
where the time goes in v5:
time: 165 us
  blocking collectives  62.2 us (38%)
  Pallas kernels  53.1 us (32%)
  waiting for transfers between devices  34.9 us (21%)
  starting transfers between devices  11.5 us (7%)
    all_to_all x1, blocking collectives, local(): lax.all_to_all(errors.reshape(128, EC, 128), BOTH, 0, 0, tiled=True)  62.2 us
    pallas_call x1, Pallas kernels, local(): call(main_body, [smem, vmem, vmem], hbm, jax.ShapeDtypeStruct((128 * EC,...  44.4 us
    all_to_all x1, waiting for transfers between devices, local(): recv = lax.all_to_all(sent, BOTH, 0, 0, tiled=True).reshape(128 * CH, 128)  34.9 us
    all_to_all x1, starting transfers between devices, local(): recv = lax.all_to_all(sent, BOTH, 0, 0, tiled=True).reshape(128 * CH, 128)  11.5 us
    pallas_call x1, Pallas kernels, local(): call(send_body, [smem, hbm, hbm, hbm, vmem, vmem, vmem], hbm, jax.ShapeDt...  5.18 us
    pallas_call x1, Pallas kernels, local(): call(place_body, [hbm], (vmem, vmem, vmem), (jax.ShapeDtypeStruct((128, 8...  3.58 us
  transfers between devices with their start and end apart: 1, of which 1 were waited for; matrix products, arithmetic and copies ran while one was open for 1% of the time, Pallas kernels for 0%

profile of v5, /device:TPU:1, one launch (start us, length us, event | category | flops | bytes accessed | tf_op | source)
XLA Modules:
  0.0 164.7 jit_solution(9183531415457315360)
XLA Ops:
  0.6 0.0 copy-start
  0.7 0.6 pad_add_fusion.place
  1.2 5.2 %shard_map.94 = f32[128,40,128]{2,1,0:T(8,128)} custom-call(s32[2]{0:T(128)} %pad_add_fusion.place, f32[512,768]{1,0:T(8,128)} %bitcast.15, s32[512,96]{1,0:T(8,128)} %bitcast.17, f32[128,768]{1,0:T(8,128)} %cent.1, s32[1,64]{1,0:T(1,128)} %bitcast.20, s32[1,64]{1,0:T(1,128)} %bitcast.21, s32[8,64]{1,0:T(8,128)} %bitcast.19), custom_call_target="tpu_custom_call" | custom-call | bytes 5242880 | tf_op jit(solution)/shard_map/pallas_call | solution.py:411
  6.4 0.0 copy-start.1
  6.4 11.5 %all-to-all-start = ((f32[128,40,128]{2,1,0:T(8,128)}), f32[128,40,128]{2,1,0:T(8,128)S(1)}, u32[]{:S(2)}, u32[]{:S(2)}) async-start(f32[128,40,128]{2,1,0:T(8,128)} %shard_map.94), calls=%async_computation | async-start | bytes 5242880 | tf_op jit(solution)/shard_map/all_to_all | solution.py:438
  18.0 0.0 copy-done
  18.0 0.1 constant_dynamic-slice_fusion
  18.1 0.7 copy.11
  18.8 0.9 select_maximum_fusion.book
  19.7 34.9 %all-to-all-done = f32[128,40,128]{2,1,0:T(8,128)S(1)} async-done(((f32[128,40,128]{2,1,0:T(8,128)}), f32[128,40,128]{2,1,0:T(8,128)S(1)}, u32[]{:S(2)}, u32[]{:S(2)}) %all-to-all-start) | async-done | bytes 2621472 | tf_op jit(solution)/shard_map/all_to_all | solution.py:438
  54.6 0.0 copy-done.1
  54.6 44.4 %shard_map.95 = f32[9216,128]{1,0:T(8,128)S(1)} custom-call(s32[2]{0:T(128)S(1)} %copy-done.1, f32[5120,128]{1,0:T(8,128)S(1)} %bitcast.14, f32[4,8,128]{2,1,0:T(8,128)S(1)} %select_maximum_fusion.book), custom_call_target="tpu_custom_call" | custom-call | flops 17179869184 | bytes 8388608 | tf_op jit(solution)/shard_map/pallas_call | solution.py:442
  98.9 62.2 %all_to_all.10.landed = f32[128,72,128]{2,1,0:T(8,128)S(1)} all-to-all(f32[128,72,128]{2,1,0:T(8,128)S(1)} %bitcast.13), channel_id=1, replica_groups=mesh['shard'=32,'grp'=4] {'shard','grp'}, dimensions={0} | all-to-all | bytes 9437184 | tf_op jit(solution)/shard_map/all_to_all | solution.py:464
  161.2 3.6 %shard_map.96 = (bf16[128,8,768]{2,1,0:T(8,128)(2,1)}, f32[128,768]{1,0:T(8,128)}, f32[256,768]{1,0:T(8,128)}) custom-call(f32[128,72,128]{2,1,0:T(8,128)S(1)} %all_to_all.10.landed), custom_call_target="tpu_custom_call" | custom-call | bytes 7340032 | tf_op jit(solution)/shard_map/pallas_call | solution.py:466
Async XLA Ops:
  0.6 17.3 %copy-start = (f32[256,768]{1,0:T(8,128)S(1)}, f32[256,768]{1,0:T(8,128)}, u32[]{:S(2)}) copy-start(f32[256,768]{1,0:T(8,128)} %param.13) | copy-start | bytes 2359300
  6.4 48.1 %copy-start.1 = (s32[2]{0:T(128)S(1)}, s32[2]{0:T(128)}, u32[]{:S(2)}) copy-start(s32[2]{0:T(128)} %pad_add_fusion.place) | copy-start | bytes 28
  6.4 48.1 %all-to-all-start = ((f32[128,40,128]{2,1,0:T(8,128)}), f32[128,40,128]{2,1,0:T(8,128)S(1)}, u32[]{:S(2)}, u32[]{:S(2)}) async-start(f32[128,40,128]{2,1,0:T(8,128)} %shard_map.94), calls=%async_computation | async-start | bytes 5242880 | tf_op jit(solution)/shard_map/all_to_all | solution.py:438
